TPU v7x, 256 devices: a whole 4x4x8 slice. The times are simulated.
256 devices in a mesh: pts: 256 (over z, y, x, core).
Axes of the slice: x: 4, y: 4, z: 8, core: 2. Of those that a mesh axis runs over, the one named last changes fastest.
Arguments:
- embeddings: bfloat16 [262144, 384], P('pts'), may hold values from -1 to 1, as said below
- site_ids: int32 [262144], P('pts'), may hold values from 0 to 63
- inv_scale: float32 [384], replicated, may hold values from 0.5 to 2
- noise: float32 [128], replicated, may hold values from 0.5 to 2
- solution: float32 [262144, 128], P('pts'), may hold values from -6 to 6
- residual: float32 [262144, 128], P('pts'), may hold values from -9 to 9, as said below
- direction: float32 [262144, 128], P('pts'), may hold values from -9 to 9, as said below
Outputs:
- new_solution: float32 [262144, 128], P('pts')
- new_residual: float32 [262144, 128], P('pts')
- new_direction: float32 [262144, 128], P('pts')
- new_norms: float32 [128], replicated
Inputs may be any that keep to these rules, and one draw needn't show every extreme that they name: `embeddings`: real values. `residual`: real values. Entries drawn independently of the embeddings; in every column the sum of direction times applied is positive.
All inputs are finite; a program needn't handle non-finite values.
Results may differ from a plain program's by a relative error of at most 0.0085.
Values may be sent and summed in bfloat16 or wider, within the bound.
A program may use at most 64 MiB of HBM per device.

v0:
```python
import math

import jax
import jax.numpy as jnp
from jax import lax
from jax.sharding import PartitionSpec as P

root_three = math.sqrt(3.0)
site_weight = 0.5


def passed_along(block, axis, distance):
    devices = range(lax.axis_size(axis))
    route = [((i - distance) % len(devices), i) for i in devices]
    return lax.ppermute(block, axis, route)


def kernel_tile(left_rows, left_norms, left_sites, right_rows, right_norms, right_sites):
    cross = jnp.einsum("pf,qf->pq", left_rows, right_rows, preferred_element_type=jnp.float32)
    squared = jnp.maximum(left_norms[:, None] + right_norms[None, :] - 2.0 * cross, 0.0)
    distance = jnp.sqrt(squared)
    matern = (1.0 + root_three * distance) * jnp.exp(-root_three * distance)
    same_site = (left_sites[:, None] == right_sites[None, :]).astype(jnp.float32)
    return (matern + site_weight * same_site).astype(jnp.bfloat16)


def row_norms(rows):
    return jnp.sum(jnp.square(rows.astype(jnp.float32)), axis=1)


def body(embeddings, site_ids, inv_scale, noise, solution, residual, direction):
    scaled = (embeddings.astype(jnp.float32) * inv_scale).astype(jnp.bfloat16)
    sq_norms = row_norms(scaled)
    dir_low = direction.astype(jnp.bfloat16)
    features = scaled.shape[1]
    payload = jnp.concatenate([scaled, dir_low], axis=1)
    players = lax.axis_size("pts")

    def partner_product(block, partner_sites):
        partner_rows = block[:, :features]
        partner_dirs = block[:, features:]
        pair_tile = kernel_tile(
            scaled, sq_norms, site_ids, partner_rows, row_norms(partner_rows), partner_sites
        )
        return (pair_tile, jnp.dot(pair_tile, partner_dirs, preferred_element_type=jnp.float32))

    below_block, below_sites = passed_along((payload, site_ids), "pts", 1)
    far_block, far_sites = passed_along((payload, site_ids), "pts", players // 2)
    self_tile = kernel_tile(scaled, sq_norms, site_ids, scaled, sq_norms, site_ids)
    products = jnp.dot(self_tile, dir_low, preferred_element_type=jnp.float32)
    lower_tile, lower_part = partner_product(below_block, below_sites)
    products = products + lower_part
    above_block, above_sites = passed_along((payload, site_ids), "pts", -1)
    upper_tile, upper_part = partner_product(above_block, above_sites)
    products = products + upper_part
    far_tile, far_part = partner_product(far_block, far_sites)
    products = products + far_part
    applied = noise * direction + products
    old_norms = lax.psum(jnp.sum(residual * residual, axis=0), "pts")
    curvature = lax.psum(jnp.sum(direction * applied, axis=0), "pts")
    step_size = old_norms / curvature
    new_residual = residual - step_size * applied
    new_norms = lax.psum(jnp.sum(new_residual * new_residual, axis=0), "pts")
    new_solution = solution + step_size * direction
    new_direction = new_residual + new_norms / old_norms * direction
    return (new_solution, new_residual, new_direction, new_norms)


def solution(mesh):
    placed = (P("pts", None), P("pts"), P(), P(), P("pts", None), P("pts", None), P("pts", None))
    return jax.shard_map(
        body,
        mesh=mesh,
        in_specs=placed,
        out_specs=(P("pts", None), P("pts", None), P("pts", None), P()),
        check_vma=False,
    )
```

profile of v0, /device:TPU:1, one launch (start us, length us, event | category | flops | bytes accessed | tf_op | source)
XLA Modules:
  0.0 238.7 jit_solution(18346727590402777129)
XLA Ops:
  0.6 1.1 convert_element_type.41
  1.8 0.1 copy-done.3
  1.9 1.0 multiply_reduce_fusion.3
  2.9 0.1 pad_maximum_fusion
  3.0 7.8 %collective-permute-start.4 = (bf16[1024,512]{1,0:T(8,128)(2,1)S(1)}, bf16[1024,512]{1,0:T(8,128)(2,1)}, u32[]{:S(2)}, u32[]{:S(2)}) collective-permute-start(bf16[1024,512]{1,0:T(8,128)(2,1)S(1)} %pad_maximum_fusion), channel_id=1, source_target_pairs={{128,0},{129,1},{130,2},{131,3},{132,4},{133,5},{134,6},{135,7},{1... | collective-permute-start | bytes 3145736 | tf_op jit(solution)/shard_map/ppermute | solution.py:15
  10.9 2.1 collective-permute-start
  12.9 0.0 copy-done.5
  12.9 0.0 collective-permute-start.1
  12.9 0.2 collective-permute-start.5
  13.1 0.4 collective-permute-start.2
  13.5 4.0 %fusion = f32[1024,128]{1,0:T(8,128)} fusion(bf16[1024,128]{1,0:T(8,128)(2,1)S(1)} %convert_element_type.41, bf16[1024,384]{1,0:T(8,128)(2,1)S(1)} %get-tuple-element.9, s32[1024]{0:T(1024)S(1)} %copy-done.5, f32[1024]{0:T(1024)S(1)} %get-tuple-element.8), kind=kOutput, calls=%fused_computation.9 | convolution fusion | flops 1086324736 | bytes 1581056 | tf_op jit(solution)/shard_map/dot_general | solution.py:50
  17.5 0.1 multiply_reduce_fusion.6
  17.7 21.6 %collective-permute-done.4 = bf16[1024,512]{1,0:T(8,128)(2,1)} collective-permute-done((bf16[1024,512]{1,0:T(8,128)(2,1)S(1)}, bf16[1024,512]{1,0:T(8,128)(2,1)}, u32[]{:S(2)}, u32[]{:S(2)}) %collective-permute-start.4) | collective-permute-done | bytes 1048608 | tf_op jit(solution)/shard_map/ppermute | solution.py:15
  39.3 17.1 %collective-permute-start.3 = (s32[1024]{0:T(1024)S(1)}, s32[1024]{0:T(1024)S(1)}, u32[]{:S(2)}, u32[]{:S(2)}) collective-permute-start(s32[1024]{0:T(1024)S(1)} %copy-done.5), channel_id=1, source_target_pairs={{1,0},{2,1},{3,2},{4,3},{5,4},{6,5},{7,6},{8,7},{9,8},{10,9},{11,1... | collective-permute-start | bytes 12296 | tf_op jit(solution)/shard_map/ppermute | solution.py:15
  56.3 1.4 multiply_reduce_fusion
  57.7 0.0 collective-permute-done.5
  57.7 4.4 %fusion.3 = f32[1024,128]{1,0:T(8,128)S(1)} fusion(bf16[1024,384]{1,0:T(8,128)(2,1)S(1)} %get-tuple-element.9, s32[1024]{0:T(1024)S(1)} %collective-permute-done.5, f32[1024]{0:T(1024)S(1)} %multiply_reduce_fusion, f32[1024]{0:T(1024)S(1)} %get-tuple-element.8, s32[1024]{0:T(1024)S(1)} %copy-done.5, bf16[1024,512]{1,0:T(8,128)(2,1)} %collective-permute-done.4), kind=kOutput, calls=%fused_computation.12 | convolution fusion | flops 1086324736 | bytes 2375680 | tf_op jit(solution)/shard_map/dot_general | solution.py:45
  62.1 0.0 collective-permute-done
  62.1 1.4 multiply_reduce_fusion.2
  63.5 0.0 copy-start
  63.5 0.0 copy-start.6
  63.5 0.0 collective-permute-done.1
  63.5 5.7 %fusion.5 = f32[1024,128]{1,0:T(8,128)} fusion(f32[1024,128]{1,0:T(8,128)} %fusion, bf16[1024,384]{1,0:T(8,128)(2,1)S(1)} %get-tuple-element.9, s32[1024]{0:T(1024)S(1)} %collective-permute-done.1, f32[1024]{0:T(1024)S(1)} %multiply_reduce_fusion.2, f32[1024]{0:T(1024)S(1)} %get-tuple-element.8, s32[1024]{0:T(1024)S(1)} %copy-done.5, ...), kind=kOutput, calls=%fused_computation.14 | convolution fusion | flops 1086455808 | bytes 2899968 | tf_op jit(solution)/shard_map/dot_general | solution.py:45
  69.2 0.0 collective-permute-done.2
  69.2 1.4 multiply_reduce_fusion.1
  70.6 0.0 collective-permute-done.3
  70.6 5.0 %multiply_reduce_fusion.5 = (f32[128]{0:T(128)S(1)}, f32[1024,128]{1,0:T(8,128)S(1)}) fusion(f32[1024,128]{1,0:T(8,128)S(1)} %copy-done, f32[1024,128]{1,0:T(8,128)S(1)} %fusion.3, f32[1024,128]{1,0:T(8,128)} %fusion.5, bf16[1024,512]{1,0:T(8,128)(2,1)} %collective-permute-done.2, bf16[1024,384]{1,0:T(8,128)(2,1)S(1)} %get-tuple-element.9, ...), kind=kOutput, calls=%fused_computation.25 | convolution fusion | flops 1087111040 | bytes 3949568 | tf_op jit(solution)/shard_map/dot_general | solution.py:45
  75.6 88.5 %all-reduce = (f32[128]{0:T(128)S(1)}, f32[128]{0:T(128)S(1)}) all-reduce(f32[128]{0:T(128)S(1)} %multiply_reduce_fusion.6, f32[128]{0:T(128)S(1)} %get-tuple-element.12), channel_id=1, replica_groups=mesh['pts'=256] {'pts'}, use_global_device_ids=true, to_apply=%region_1.0 | all-reduce | flops 256 | bytes 2048 | tf_op jit(solution)/shard_map/psum | solution.py:59
  164.1 0.2 multiply_reduce_fusion.4
  164.3 73.3 %psum.23 = f32[128]{0:T(128)S(1)} all-reduce(f32[128]{0:T(128)S(1)} %get-tuple-element.6), channel_id=1, replica_groups=mesh['pts'=256] {'pts'}, use_global_device_ids=true, to_apply=%region_9.0 | all-reduce | flops 128 | bytes 1024 | tf_op jit(solution)/shard_map/psum | solution.py:63
  237.6 1.1 multiply_add_fusion
  238.7 0.0 copy-done.7
  (13 shorter events, 0.0 us)
Async XLA Ops:
  0.6 1.3 copy-start.3
  2.9 10.0 %copy-start.5 = (s32[1024]{0:T(1024)S(1)}, s32[1024]{0:T(1024)}, u32[]{:S(2)}) copy-start(s32[1024]{0:T(1024)} %param.8) | copy-start | bytes 12292
  3.0 36.3 %collective-permute-start.4 = (bf16[1024,512]{1,0:T(8,128)(2,1)S(1)}, bf16[1024,512]{1,0:T(8,128)(2,1)}, u32[]{:S(2)}, u32[]{:S(2)}) collective-permute-start(bf16[1024,512]{1,0:T(8,128)(2,1)S(1)} %pad_maximum_fusion), channel_id=1, source_target_pairs={{128,0},{129,1},{130,2},{131,3},{132,4},{133,5},{134,6},{135,7},{1... | collective-permute-start | bytes 3145736 | tf_op jit(solution)/shard_map/ppermute | solution.py:15
  10.9 51.2 %collective-permute-start = (bf16[1024,512]{1,0:T(8,128)(2,1)S(1)}, bf16[1024,512]{1,0:T(8,128)(2,1)}, u32[]{:S(2)}, u32[]{:S(2)}) collective-permute-start(bf16[1024,512]{1,0:T(8,128)(2,1)S(1)} %pad_maximum_fusion), channel_id=1, source_target_pairs={{255,0},{0,1},{1,2},{2,3},{3,4},{4,5},{5,6},{6,7},{7,8},{8,9},{9,1... | collective-permute-start | bytes 3145736 | tf_op jit(solution)/shard_map/ppermute | solution.py:15
  12.9 50.6 %collective-permute-start.1 = (s32[1024]{0:T(1024)S(1)}, s32[1024]{0:T(1024)S(1)}, u32[]{:S(2)}, u32[]{:S(2)}) collective-permute-start(s32[1024]{0:T(1024)S(1)} %copy-done.5), channel_id=1, source_target_pairs={{255,0},{0,1},{1,2},{2,3},{3,4},{4,5},{5,6},{6,7},{7,8},{8,9},{9,1... | collective-permute-start | bytes 12296 | tf_op jit(solution)/shard_map/ppermute | solution.py:15
  12.9 44.8 %collective-permute-start.5 = (s32[1024]{0:T(1024)S(1)}, s32[1024]{0:T(1024)S(1)}, u32[]{:S(2)}, u32[]{:S(2)}) collective-permute-start(s32[1024]{0:T(1024)S(1)} %copy-done.5), channel_id=1, source_target_pairs={{128,0},{129,1},{130,2},{131,3},{132,4},{133,5},{134,6},{135,7},{1... | collective-permute-start | bytes 12296 | tf_op jit(solution)/shard_map/ppermute | solution.py:15
  13.1 56.1 %collective-permute-start.2 = (bf16[1024,512]{1,0:T(8,128)(2,1)S(1)}, bf16[1024,512]{1,0:T(8,128)(2,1)}, u32[]{:S(2)}, u32[]{:S(2)}) collective-permute-start(bf16[1024,512]{1,0:T(8,128)(2,1)S(1)} %pad_maximum_fusion), channel_id=1, source_target_pairs={{1,0},{2,1},{3,2},{4,3},{5,4},{6,5},{7,6},{8,7},{9,8},{10,9},{11,1... | collective-permute-start | bytes 3145736 | tf_op jit(solution)/shard_map/ppermute | solution.py:15
  13.5 4.0 %copy-start.2 = (f32[1024,128]{1,0:T(8,128)S(1)}, f32[1024,128]{1,0:T(8,128)}, u32[]{:S(2)}) copy-start(f32[1024,128]{1,0:T(8,128)} %param.12) | copy-start | bytes 1572868
  39.3 31.3 %collective-permute-start.3 = (s32[1024]{0:T(1024)S(1)}, s32[1024]{0:T(1024)S(1)}, u32[]{:S(2)}, u32[]{:S(2)}) collective-permute-start(s32[1024]{0:T(1024)S(1)} %copy-done.5), channel_id=1, source_target_pairs={{1,0},{2,1},{3,2},{4,3},{5,4},{6,5},{7,6},{8,7},{9,8},{10,9},{11,1... | collective-permute-start | bytes 12296 | tf_op jit(solution)/shard_map/ppermute | solution.py:15
  63.5 7.1 %copy-start = (f32[1024,128]{1,0:T(8,128)S(1)}, f32[1024,128]{1,0:T(8,128)}, u32[]{:S(2)}) copy-start(f32[1024,128]{1,0:T(8,128)} %param.13) | copy-start | bytes 1572868
  63.5 7.1 %copy-start.6 = (f32[128]{0:T(128)S(1)}, f32[128]{0:T(128)}, u32[]{:S(2)}) copy-start(f32[128]{0:T(128)} %param.10) | copy-start | bytes 1540
  75.6 162.0 %copy-start.4 = (f32[1024,128]{1,0:T(8,128)S(1)}, f32[1024,128]{1,0:T(8,128)}, u32[]{:S(2)}) copy-start(f32[1024,128]{1,0:T(8,128)} %param.11) | copy-start | bytes 1572868
  164.2 74.4 %copy-start.1 = (f32[1024,128]{1,0:T(8,128)}, f32[1024,128]{1,0:T(8,128)S(1)}, u32[]{:S(2)}) copy-start(f32[1024,128]{1,0:T(8,128)S(1)} %get-tuple-element.7) | copy-start | bytes 1572868
  237.6 1.1 copy-start.7
where the time goes:
time: 239 us
  blocking collectives  162 us (68%)
  starting transfers between devices  27.6 us (12%)
  waiting for transfers between devices  21.6 us (9%)
  matrix products  19.1 us (8%)
  other arithmetic  7.73 us (3%)
    psum x1, blocking collectives, body(): old_norms = lax.psum(jnp.sum(residual * residual, axis=0), 'pts')  88.5 us
    psum x1, blocking collectives, body(): new_norms = lax.psum(jnp.sum(new_residual * new_residual, axis=0), 'pts')  73.3 us
    ppermute x6, starting transfers between devices, passed_along(): return lax.ppermute(block, axis, route)  27.6 us
    ppermute x6, waiting for transfers between devices, passed_along(): return lax.ppermute(block, axis, route)  21.6 us
    dot_general x3, matrix products, partner_product(): jnp.dot(pair_tile, partner_dirs, preferred_element_type=jnp.float32)  15.1 us
    reduce_sum x4, other arithmetic, row_norms(): return jnp.sum(jnp.square(rows.astype(jnp.float32)), axis=1)  5.06 us
  transfers between devices with their start and end apart: 6, of which 1 were waited for; matrix products, arithmetic and copies ran while one was open for 8% of the time, Pallas kernels for 0%

commit v1 on v0

v1 whole, which is shorter than its diff:
```python
import functools
import math

import jax
import jax.numpy as jnp
from jax import lax
from jax.experimental import pallas as pl
from jax.experimental.pallas import tpu as pltpu
from jax.sharding import PartitionSpec as P

root_three = math.sqrt(3.0)
site_weight = 0.5
sites = 64

MESH = pl.DeviceIdType.MESH
ZS, YS, XS, CS = 8, 4, 4, 2
PLANE = YS * XS * CS
PTS = ZS * PLANE
ROWS = 1024
F = 384
R = 128
CHUNK = 256
CHUNKS = ROWS // CHUNK
f32 = jnp.float32
bf16 = jnp.bfloat16


def dot(a, b):
    return jnp.dot(a, b, preferred_element_type=f32)


def matern(left, right, left_norms, right_norms):
    cross = lax.dot_general(left, right, (((1,), (1,)), ((), ())), preferred_element_type=f32)
    squared = jnp.maximum(cross + left_norms + right_norms, 1e-30)
    distance = squared * lax.rsqrt(squared)
    decay = jnp.exp2(distance * (-root_three * math.log2(math.e)))
    return ((1.0 + root_three * distance) * decay).astype(bf16)


def one_hot(ids):
    rows = lax.broadcasted_iota(jnp.int32, (2 * sites, ids.shape[1]), 0) % sites
    return (rows.astype(f32) == ids).astype(bf16)


def split_halves(totals):
    high = totals.astype(bf16)
    low = (totals - high.astype(f32)).astype(bf16)
    rows = lax.broadcasted_iota(jnp.int32, totals.shape, 0)
    return jnp.where(rows < sites, high, low)


def kernel(
    emb_hbm, dir_hbm, res_hbm, ids_ref, scale_ref, noise_ref,
    applied_ref, sums_ref,
    emb, direction, residual, own, left, norm_col, dir_t, own_meta,
    near, near_meta, far, far_meta, ret_out, ret_in, acc, totals, first, second,
    load_sem, near_send, near_recv, near_meta_send, near_meta_recv,
    far_send, far_recv, far_meta_send, far_meta_recv,
    ret_send, ret_recv, sum_send, sum_recv,
):
    me = lax.axis_index("pts")
    core = me % CS
    plane = me // PLANE
    spot = (me // CS) % (YS * XS)

    twin = me + 1 - 2 * core
    step = 2 * core - 1
    beside = (me + step + PTS) % PTS
    opposite = (me + PTS // 2) % PTS
    sends = (me // (PTS // 2) + me) % 2 == 0
    receives = jnp.logical_not(sends)

    column_place = plane * CS + core
    column = [
        ((plane + dz) % ZS) * PLANE + spot * CS + (core + dc) % CS
        for dz in range(ZS) for dc in range(CS) if dz or dc
    ]
    layer = [
        plane * PLANE + ((spot + k) % (YS * XS)) * CS + core for k in range(1, YS * XS)
    ]

    loads = [
        pltpu.make_async_copy(src, dst, load_sem.at[k])
        for k, (src, dst) in enumerate(((emb_hbm, emb), (dir_hbm, direction), (res_hbm, residual)))
    ]
    for load in loads:
        load.start()

    barrier = pltpu.get_barrier_semaphore()
    partners = [beside] + column + layer
    for other in partners:
        pl.semaphore_signal(barrier, inc=1, device_id=(other,), device_id_type=MESH)

    def send(src, dst, send_sem, recv_sem, other):
        return pltpu.make_async_remote_copy(
            src_ref=src, dst_ref=dst, send_sem=send_sem, recv_sem=recv_sem,
            device_id=(other,), device_id_type=MESH,
        )

    def rows_of(k):
        return pl.ds(k * CHUNK, CHUNK)

    far_copies = [
        send(own.at[rows_of(k)], far.at[rows_of(k)], far_send.at[k], far_recv.at[k], opposite)
        for k in range(CHUNKS)
    ]
    near_copies = [
        [
            send(own.at[rows_of(k)], near.at[n, rows_of(k)], near_send.at[n, k], near_recv.at[n, k], other)
            for k in range(CHUNKS)
        ]
        for n, other in enumerate((twin, beside))
    ]
    far_meta_copy = send(own_meta, far_meta, far_meta_send, far_meta_recv, opposite)
    near_meta_copies = [
        send(own_meta, near_meta.at[n], near_meta_send.at[n], near_meta_recv.at[n], other)
        for n, other in enumerate((twin, beside))
    ]
    ret_copies = [
        send(ret_out.at[k], ret_in.at[k], ret_send.at[k], ret_recv.at[k], opposite)
        for k in range(CHUNKS)
    ]

    loads[0].wait()
    loads[1].wait()
    for k in range(CHUNKS):
        rows = rows_of(k)
        scaled = (emb[rows, :].astype(f32) * scale_ref[...]).astype(bf16)
        own[rows, :F] = scaled
        own[rows, F:] = direction[rows, :].astype(bf16)
        wide = scaled.astype(f32)
        left[rows, :] = (-2.0 * wide).astype(bf16)
        norm_col[rows, :] = jnp.broadcast_to(jnp.sum(wide * wide, axis=1, keepdims=True), (CHUNK, 128))
        if k == 0:
            pl.semaphore_wait(barrier, len(partners))

        @pl.when(sends)
        def _():
            far_copies[k].start()

        near_copies[0][k].start()
        near_copies[1][k].start()
    own_meta[0:1, :] = norm_col[...].T[0:1, :]
    own_meta[1:2, :] = ids_ref[...].astype(f32)

    @pl.when(sends)
    def _():
        far_meta_copy.start()

    for copy in near_meta_copies:
        copy.start()

    def add_block(block, meta):
        def some_rows(t, carry):
            rows = pl.ds(pl.multiple_of(t * CHUNK, CHUNK), CHUNK)
            tile = matern(left[rows, :], block[:, :F], norm_col[rows, 0:1], meta[0:1, :])
            acc[rows, :] += dot(tile, block[:, F:])
            return carry

        lax.fori_loop(0, CHUNKS, some_rows, 0)
        return dot(one_hot(meta[1:2, :]), block[:, F:])

    acc[...] = noise_ref[...] * direction[...]
    dir_t[...] = direction[...].T.astype(bf16)
    own_totals = add_block(own, own_meta)
    totals[...] = own_totals
    own_halves_t = split_halves(own_totals).astype(f32).T.astype(bf16)

    near_meta_copies[0].wait_recv()
    for copy in near_copies[0]:
        copy.wait_recv()
    totals[...] += add_block(near.at[0], near_meta.at[0])

    def far_chunk(k):
        far_copies[k].wait_recv()
        rows = rows_of(k)
        tile = matern(left[...], far[rows, :F], norm_col[:, 0:1], far_meta[0:1, rows])
        spots = one_hot(far_meta[1:2, rows])
        back = dot(dir_t[...], tile) + site_weight * dot(own_halves_t, spots)
        ret_out[k] = back.astype(bf16)
        ret_copies[k].start()
        acc[...] += dot(tile, far[rows, F:])
        totals[...] += dot(spots, far[rows, F:])

    def take_back(k):
        ret_copies[k].wait_recv()
        acc[rows_of(k), :] += ret_in[k].astype(f32).T

    @pl.when(receives)
    def _():
        far_meta_copy.wait_recv()
        far_chunk(0)

    near_meta_copies[1].wait_recv()
    for copy in near_copies[1]:
        copy.wait_recv()
    totals[...] += add_block(near.at[1], near_meta.at[1])

    loads[2].wait()
    sums_ref[0:1, :] = jnp.sum(residual[...] * residual[...], axis=0, keepdims=True)

    @pl.when(receives)
    def _():
        for k in range(1, CHUNKS):
            far_chunk(k)

    @pl.when(sends)
    def _():
        for k in range(CHUNKS):
            take_back(k)

    spread = one_hot(own_meta[1:2, :]).astype(f32).T.astype(bf16)
    applied = acc[...] + site_weight * dot(spread, split_halves(totals[...]))
    applied_ref[...] = applied
    sums_ref[1:2, :] = jnp.sum(direction[...] * applied, axis=0, keepdims=True)
    sums_ref[2:3, :] = jnp.sum(residual[...] * applied, axis=0, keepdims=True)
    sums_ref[3:4, :] = jnp.sum(applied * applied, axis=0, keepdims=True)

    def gather_sum(stage, slots, place, others):
        slots[place] = sums_ref[...]
        for other in others:
            send(slots.at[place], slots.at[place], sum_send.at[stage], sum_recv.at[stage], other).start()
        rest = slots.at[pl.ds(0, len(others))]
        every = send(rest, rest, sum_send.at[stage], sum_recv.at[stage], others[0])
        every.wait_recv()
        sums_ref[...] = jnp.sum(slots[...], axis=0)
        return every

    stages = [gather_sum(0, first, column_place, column), gather_sum(1, second, spot, layer)]
    for stage in stages:
        stage.wait_send()

    @pl.when(sends)
    def _():
        far_meta_copy.wait_send()
        for copy in far_copies:
            copy.wait_send()

    @pl.when(receives)
    def _():
        for copy in ret_copies:
            copy.wait_send()

    for copy in near_meta_copies + near_copies[0] + near_copies[1]:
        copy.wait_send()


def body(embeddings, site_ids, inv_scale, noise, solution, residual, direction):
    vmem = pl.BlockSpec(memory_space=pltpu.VMEM)
    anywhere = pl.BlockSpec(memory_space=pl.ANY)
    dma = pltpu.SemaphoreType.DMA
    applied, sums = pl.pallas_call(
        kernel,
        out_shape=(
            jax.ShapeDtypeStruct((ROWS, R), f32),
            jax.ShapeDtypeStruct((4, R), f32),
        ),
        in_specs=[anywhere] * 3 + [vmem] * 3,
        out_specs=[vmem] * 2,
        scratch_shapes=[
            pltpu.VMEM((ROWS, F), bf16),
            pltpu.VMEM((ROWS, R), f32),
            pltpu.VMEM((ROWS, R), f32),
            pltpu.VMEM((ROWS, F + R), bf16),
            pltpu.VMEM((ROWS, F), bf16),
            pltpu.VMEM((ROWS, 128), f32),
            pltpu.VMEM((R, ROWS), bf16),
            pltpu.VMEM((2, ROWS), f32),
            pltpu.VMEM((2, ROWS, F + R), bf16),
            pltpu.VMEM((2, 2, ROWS), f32),
            pltpu.VMEM((ROWS, F + R), bf16),
            pltpu.VMEM((2, ROWS), f32),
            pltpu.VMEM((CHUNKS, R, CHUNK), bf16),
            pltpu.VMEM((CHUNKS, R, CHUNK), bf16),
            pltpu.VMEM((ROWS, R), f32),
            pltpu.VMEM((2 * sites, R), f32),
            pltpu.VMEM((ZS * CS, 4, R), f32),
            pltpu.VMEM((YS * XS, 4, R), f32),
            dma((3,)),
            dma((2, CHUNKS)),
            dma((2, CHUNKS)),
            dma((2,)),
            dma((2,)),
            dma((CHUNKS,)),
            dma((CHUNKS,)),
            dma,
            dma,
            dma((CHUNKS,)),
            dma((CHUNKS,)),
            dma((2,)),
            dma((2,)),
        ],
        compiler_params=pltpu.CompilerParams(
            collective_id=0, has_side_effects=True, vmem_limit_bytes=48 * 1024 * 1024
        ),
        name="cg_products",
    )(embeddings, direction, residual, site_ids.reshape(1, ROWS), inv_scale.reshape(1, F), noise.reshape(1, R))
    old_norms, curvature, mixed, applied_norms = sums
    step_size = old_norms / curvature
    new_norms = jnp.maximum(old_norms - 2.0 * step_size * mixed + step_size * step_size * applied_norms, 0.0)
    new_solution = solution + step_size * direction
    new_residual = residual - step_size * applied
    new_direction = new_residual + new_norms / old_norms * direction
    return (new_solution, new_residual, new_direction, new_norms)


def solution(mesh):
    placed = (P("pts", None), P("pts"), P(), P(), P("pts", None), P("pts", None), P("pts", None))
    return jax.shard_map(
        body,
        mesh=mesh,
        in_specs=placed,
        out_specs=(P("pts", None), P("pts", None), P("pts", None), P()),
        check_vma=False,
    )
```

time: 239 us -> 77.9 us (0.33)
  blocking collectives: 162 us -> 0 us
  Pallas kernels: 0 us -> 70.6 us
  starting transfers between devices: 27.6 us -> 0 us
  waiting for transfers between devices: 21.6 us -> 0 us
  matrix products: 19.1 us -> 0 us
  other arithmetic: 7.73 us -> 1.81 us
  local copies, waits for them, and re-layouts: 0.17 us -> 4.54 us
    psum x2 -> x0, blocking collectives: 162 us -> none  [the longest x1 88.5 us: body(): old_norms = lax.psum(jnp.sum(residual * residual, axis=0), 'pts')]
    pallas_call x0 -> x1, Pallas kernels: none -> 70.6 us  [body(): pl.pallas_call(kernel, out_shape=(jax.ShapeDtypeStruct((ROWS, R), f32), j...]
    ppermute x6 -> x0, starting transfers between devices: 27.6 us -> none  [passed_along(): return lax.ppermute(block, axis, route)]
    ppermute x6 -> x0, waiting for transfers between devices: 21.6 us -> none  [passed_along(): return lax.ppermute(block, axis, route)]
    dot_general x4 -> x0, matrix products: 19.1 us -> none  [the longest x3 15.1 us: partner_product(): jnp.dot(pair_tile, partner_dirs, preferred_element_type=jnp.float32)]
    reduce_sum x6 -> x0, other arithmetic: 5.38 us -> none  [the longest x4 5.06 us: row_norms(): return jnp.sum(jnp.square(rows.astype(jnp.float32)), axis=1)]
    unnamed x16 -> x14, local copies, waits for them, and re-layouts: 0.17 us -> 4.54 us
  transfers between devices with their start and end apart: 6 -> 0, of which waited for: 1 -> 0; matrix products, arithmetic and copies ran while one was open for 8% -> 0% of each run, Pallas kernels for 0% -> 0%
where the time goes in v1:
time: 77.9 us; the launch traced here: 77.6 us
  Pallas kernels  70.6 us (91%)
  local copies, waits for them, and re-layouts  4.54 us (6%)
  other arithmetic  1.81 us (2%)
    pallas_call x1, Pallas kernels, body(): pl.pallas_call(kernel, out_shape=(jax.ShapeDtypeStruct((ROWS, R), f32), j...  70.6 us
    unnamed x14, local copies, waits for them, and re-layouts  4.54 us

profile of v1, /device:TPU:1, one launch (start us, length us, event | category | flops | bytes accessed | tf_op | source)
XLA Modules:
  0.0 77.6 jit_solution(2337435137627766665)
XLA Ops:
  0.6 0.0 copy-start.6
  0.6 0.0 copy-start.3
  0.7 0.7 copy-done.6
  1.3 0.0 copy-start.4
  1.3 0.0 copy-done.3
  1.3 0.6 copy-done.4
  2.0 0.0 copy-start
  2.0 1.0 %copy-done = f32[1024,128]{1,0:T(8,128)S(1)} copy-done((f32[1024,128]{1,0:T(8,128)S(1)}, f32[1024,128]{1,0:T(8,128)}, u32[]{:S(2)}) %copy-start) | copy-done | bytes 524312
  3.0 0.0 copy-start.1
  3.0 1.0 %copy-done.1 = f32[1024,128]{1,0:T(8,128)S(1)} copy-done((f32[1024,128]{1,0:T(8,128)S(1)}, f32[1024,128]{1,0:T(8,128)}, u32[]{:S(2)}) %copy-start.1) | copy-done | bytes 524312
  4.1 0.0 copy-start.2
  4.1 1.1 %copy-done.2 = bf16[1024,384]{1,0:T(8,128)(2,1)S(1)} copy-done((bf16[1024,384]{1,0:T(8,128)(2,1)S(1)}, bf16[1024,384]{1,0:T(8,128)(2,1)}, u32[]{:S(2)}) %copy-start.2) | copy-done | bytes 786456
  5.2 0.0 copy-start.5
  5.2 70.6 %cg_products.1 = (f32[1024,128]{1,0:T(8,128)S(1)}, f32[4,128]{1,0:T(4,128)S(1)}) custom-call(bf16[1024,384]{1,0:T(8,128)(2,1)S(1)} %copy-done.2, f32[1024,128]{1,0:T(8,128)S(1)} %copy-done, f32[1024,128]{1,0:T(8,128)S(1)} %copy-done.1, s32[1,1024]{1,0:T(1,128)S(1)} %bitcast.26, f32[1,384]{1,0:T(1,128)S(1)} %reshape.18.scale_ref, f32[1,128]{1,0:T(1,128)S(1)} %bitcast.27), custom_call_target="tpu_custom_call" | custom-call | tf_op jit(solution)/shard_map/cg_products/pallas_call | solution.py:252
  75.8 0.5 fusion.1
  76.4 0.0 copy-done.5
  76.4 1.3 %multiply_add_fusion = (f32[1024,128]{1,0:T(8,128)}, f32[1024,128]{1,0:T(8,128)}, f32[1024,128]{1,0:T(8,128)}) fusion(f32[1024,128]{1,0:T(8,128)S(1)} %copy-done, f32[128]{0:T(128)S(1)} %get-tuple-element.10, f32[1024,128]{1,0:T(8,128)S(1)} %copy-done.1, f32[1024,128]{1,0:T(8,128)S(1)} %get-tuple-element.7, f32[128]{0:T(128)S(1)} %bitcast.28, ...), kind=kLoop, calls=%fused_computation | loop fusion | flops 786432 | bytes 3671040 | tf_op jit(solution)/shard_map/add | solution.py:303
  (2 shorter events, 0.0 us)
Async XLA Ops:
  0.6 0.7 copy-start.6
  0.6 0.7 copy-start.3
  1.3 0.7 copy-start.4
  2.0 1.0 %copy-start = (f32[1024,128]{1,0:T(8,128)S(1)}, f32[1024,128]{1,0:T(8,128)}, u32[]{:S(2)}) copy-start(f32[1024,128]{1,0:T(8,128)} %dir_hbm.1) | copy-start | bytes 1572868
  3.0 1.0 %copy-start.1 = (f32[1024,128]{1,0:T(8,128)S(1)}, f32[1024,128]{1,0:T(8,128)}, u32[]{:S(2)}) copy-start(f32[1024,128]{1,0:T(8,128)} %res_hbm.1) | copy-start | bytes 1572868
  4.1 1.1 %copy-start.2 = (bf16[1024,384]{1,0:T(8,128)(2,1)S(1)}, bf16[1024,384]{1,0:T(8,128)(2,1)}, u32[]{:S(2)}) copy-start(bf16[1024,384]{1,0:T(8,128)(2,1)} %emb_hbm.1) | copy-start | bytes 2359300
  5.2 71.2 %copy-start.5 = (f32[1024,128]{1,0:T(8,128)S(1)}, f32[1024,128]{1,0:T(8,128)}, u32[]{:S(2)}) copy-start(f32[1024,128]{1,0:T(8,128)} %param.11) | copy-start | bytes 1572868

commit v2 on v1

--- a/solution.py
+++ b/solution.py
@@ -21,6 +21,8 @@
 R = 128
 CHUNK = 256
 CHUNKS = ROWS // CHUNK
+SPOTS = YS * XS
+PIECE = ROWS // SPOTS
 f32 = jnp.float32
 bf16 = jnp.bfloat16
 
@@ -50,18 +52,20 @@
 
 
 def kernel(
-    emb_hbm, dir_hbm, res_hbm, ids_ref, scale_ref, noise_ref,
+    emb_hbm, dir_hbm, res_hbm, ids_hbm, scale_hbm, noise_hbm,
     applied_ref, sums_ref,
-    emb, direction, residual, own, left, norm_col, dir_t, own_meta,
-    near, near_meta, far, far_meta, ret_out, ret_in, acc, totals, first, second,
+    emb, direction, residual, ids_ref, scale_ref, noise_ref, own, left, norm_col, dir_t, own_meta,
+    near, near_meta, relay, far, far_meta, ret_out, ret_in, acc, totals, first, second,
     load_sem, near_send, near_recv, near_meta_send, near_meta_recv,
-    far_send, far_recv, far_meta_send, far_meta_recv,
+    relay_send, relay_recv, far_send, far_recv, far_meta_send, far_meta_recv,
     ret_send, ret_recv, sum_send, sum_recv,
 ):
     me = lax.axis_index("pts")
     core = me % CS
     plane = me // PLANE
-    spot = (me // CS) % (YS * XS)
+    spot = (me // CS) % SPOTS
+    place = spot + core * (SPOTS - 1 - 2 * spot)
+    at_edge = place == 0
 
     twin = me + 1 - 2 * core
     step = 2 * core - 1
@@ -69,6 +73,14 @@
     opposite = (me + PTS // 2) % PTS
     sends = (me // (PTS // 2) + me) % 2 == 0
     receives = jnp.logical_not(sends)
+    next_plane = ((plane + step + ZS) % ZS) * PLANE
+
+    def at_place(base, p, c):
+        return base + (p + c * (SPOTS - 1 - 2 * p)) * CS + c
+
+    relays = [at_place(next_plane, p, 1 - core) for p in range(SPOTS)]
+    next_edge = relays[0]
+    own_edge = at_place(plane * PLANE, 0, core)
 
     column_place = plane * CS + core
     column = [
@@ -76,12 +88,17 @@
         for dz in range(ZS) for dc in range(CS) if dz or dc
     ]
     layer = [
-        plane * PLANE + ((spot + k) % (YS * XS)) * CS + core for k in range(1, YS * XS)
+        plane * PLANE + ((spot + k) % SPOTS) * CS + core for k in range(1, SPOTS)
     ]
 
     loads = [
         pltpu.make_async_copy(src, dst, load_sem.at[k])
-        for k, (src, dst) in enumerate(((emb_hbm, emb), (dir_hbm, direction), (res_hbm, residual)))
+        for k, (src, dst) in enumerate(
+            (
+                (emb_hbm, emb), (dir_hbm, direction), (scale_hbm, scale_ref),
+                (ids_hbm, ids_ref), (noise_hbm, noise_ref), (res_hbm, residual),
+            )
+        )
     ]
     for load in loads:
         load.start()
@@ -90,6 +107,10 @@
     partners = [beside] + column + layer
     for other in partners:
         pl.semaphore_signal(barrier, inc=1, device_id=(other,), device_id_type=MESH)
+
+    @pl.when(jnp.logical_not(at_edge))
+    def _():
+        pl.semaphore_signal(barrier, inc=1, device_id=(next_edge,), device_id_type=MESH)
 
     def send(src, dst, send_sem, recv_sem, other):
         return pltpu.make_async_remote_copy(
@@ -104,13 +125,30 @@
         send(own.at[rows_of(k)], far.at[rows_of(k)], far_send.at[k], far_recv.at[k], opposite)
         for k in range(CHUNKS)
     ]
-    near_copies = [
-        [
-            send(own.at[rows_of(k)], near.at[n, rows_of(k)], near_send.at[n, k], near_recv.at[n, k], other)
-            for k in range(CHUNKS)
-        ]
+    twin_copies = [
+        send(own.at[rows_of(k)], near.at[0, rows_of(k)], near_send.at[0], near_recv.at[0], twin)
+        for k in range(CHUNKS)
+    ]
+    beside_copies = [
+        send(own.at[rows_of(k)], near.at[1, rows_of(k)], near_send.at[1], near_recv.at[1], beside)
+        for k in range(CHUNKS)
+    ]
+    near_whole = [
+        send(own, near.at[n], near_send.at[n], near_recv.at[n], other)
         for n, other in enumerate((twin, beside))
     ]
+
+    def piece_of(p):
+        return pl.ds(p * PIECE, PIECE)
+
+    def edge_copy(p):
+        if p == 0:
+            return send(own.at[piece_of(0)], near.at[1, piece_of(0)], near_send.at[1], near_recv.at[1], next_edge)
+        return send(own.at[piece_of(p)], relay, near_send.at[1], relay_recv, relays[p])
+
+    held_rows = pl.ds(pl.multiple_of(place * PIECE, PIECE), PIECE)
+    relay_copy = send(relay, near.at[1, held_rows], relay_send, near_recv.at[1], own_edge)
+    relay_in = send(relay, relay, relay_send, relay_recv, own_edge)
     far_meta_copy = send(own_meta, far_meta, far_meta_send, far_meta_recv, opposite)
     near_meta_copies = [
         send(own_meta, near_meta.at[n], near_meta_send.at[n], near_meta_recv.at[n], other)
@@ -121,27 +159,37 @@
         for k in range(CHUNKS)
     ]
 
-    loads[0].wait()
-    loads[1].wait()
+    for load in loads[:3]:
+        load.wait()
     for k in range(CHUNKS):
         rows = rows_of(k)
-        scaled = (emb[rows, :].astype(f32) * scale_ref[...]).astype(bf16)
+        scaled = (emb[rows, :].astype(f32) * scale_ref[...].reshape(1, F)).astype(bf16)
         own[rows, :F] = scaled
         own[rows, F:] = direction[rows, :].astype(bf16)
         wide = scaled.astype(f32)
         left[rows, :] = (-2.0 * wide).astype(bf16)
         norm_col[rows, :] = jnp.broadcast_to(jnp.sum(wide * wide, axis=1, keepdims=True), (CHUNK, 128))
         if k == 0:
-            pl.semaphore_wait(barrier, len(partners))
+            pl.semaphore_wait(barrier, len(partners) + jnp.where(at_edge, SPOTS - 1, 0))
 
         @pl.when(sends)
         def _():
             far_copies[k].start()
 
-        near_copies[0][k].start()
-        near_copies[1][k].start()
+        twin_copies[k].start()
+
+        @pl.when(at_edge)
+        def _():
+            for p in range(k * CHUNK // PIECE, (k + 1) * CHUNK // PIECE):
+                edge_copy(p).start()
+
+        @pl.when(jnp.logical_not(at_edge))
+        def _():
+            beside_copies[k].start()
+
+    loads[3].wait()
     own_meta[0:1, :] = norm_col[...].T[0:1, :]
-    own_meta[1:2, :] = ids_ref[...].astype(f32)
+    own_meta[1:2, :] = ids_ref[...].reshape(1, ROWS).astype(f32)
 
     @pl.when(sends)
     def _():
@@ -160,16 +208,21 @@
         lax.fori_loop(0, CHUNKS, some_rows, 0)
         return dot(one_hot(meta[1:2, :]), block[:, F:])
 
-    acc[...] = noise_ref[...] * direction[...]
+    loads[4].wait()
+    acc[...] = noise_ref[...].reshape(1, R) * direction[...]
     dir_t[...] = direction[...].T.astype(bf16)
     own_totals = add_block(own, own_meta)
     totals[...] = own_totals
     own_halves_t = split_halves(own_totals).astype(f32).T.astype(bf16)
 
     near_meta_copies[0].wait_recv()
-    for copy in near_copies[0]:
-        copy.wait_recv()
+    near_whole[0].wait_recv()
     totals[...] += add_block(near.at[0], near_meta.at[0])
+
+    @pl.when(jnp.logical_not(at_edge))
+    def _():
+        relay_in.wait_recv()
+        relay_copy.start()
 
     def far_chunk(k):
         far_copies[k].wait_recv()
@@ -192,11 +245,10 @@
         far_chunk(0)
 
     near_meta_copies[1].wait_recv()
-    for copy in near_copies[1]:
-        copy.wait_recv()
+    near_whole[1].wait_recv()
     totals[...] += add_block(near.at[1], near_meta.at[1])
 
-    loads[2].wait()
+    loads[5].wait()
     sums_ref[0:1, :] = jnp.sum(residual[...] * residual[...], axis=0, keepdims=True)
 
     @pl.when(receives)
@@ -216,10 +268,10 @@
     sums_ref[2:3, :] = jnp.sum(residual[...] * applied, axis=0, keepdims=True)
     sums_ref[3:4, :] = jnp.sum(applied * applied, axis=0, keepdims=True)
 
-    def gather_sum(stage, slots, place, others):
-        slots[place] = sums_ref[...]
+    def gather_sum(stage, slots, slot, others):
+        slots[slot] = sums_ref[...]
         for other in others:
-            send(slots.at[place], slots.at[place], sum_send.at[stage], sum_recv.at[stage], other).start()
+            send(slots.at[slot], slots.at[slot], sum_send.at[stage], sum_recv.at[stage], other).start()
         rest = slots.at[pl.ds(0, len(others))]
         every = send(rest, rest, sum_send.at[stage], sum_recv.at[stage], others[0])
         every.wait_recv()
@@ -241,13 +293,17 @@
         for copy in ret_copies:
             copy.wait_send()
 
-    for copy in near_meta_copies + near_copies[0] + near_copies[1]:
+    @pl.when(jnp.logical_not(at_edge))
+    def _():
+        relay_copy.wait_send()
+
+    for copy in near_meta_copies + near_whole:
         copy.wait_send()
 
 
 def body(embeddings, site_ids, inv_scale, noise, solution, residual, direction):
     vmem = pl.BlockSpec(memory_space=pltpu.VMEM)
-    anywhere = pl.BlockSpec(memory_space=pl.ANY)
+    hbm = pl.BlockSpec(memory_space=pltpu.HBM)
     dma = pltpu.SemaphoreType.DMA
     applied, sums = pl.pallas_call(
         kernel,
@@ -255,12 +311,15 @@
             jax.ShapeDtypeStruct((ROWS, R), f32),
             jax.ShapeDtypeStruct((4, R), f32),
         ),
-        in_specs=[anywhere] * 3 + [vmem] * 3,
+        in_specs=[hbm] * 6,
         out_specs=[vmem] * 2,
         scratch_shapes=[
             pltpu.VMEM((ROWS, F), bf16),
             pltpu.VMEM((ROWS, R), f32),
             pltpu.VMEM((ROWS, R), f32),
+            pltpu.VMEM((ROWS,), jnp.int32),
+            pltpu.VMEM((F,), f32),
+            pltpu.VMEM((R,), f32),
             pltpu.VMEM((ROWS, F + R), bf16),
             pltpu.VMEM((ROWS, F), bf16),
             pltpu.VMEM((ROWS, 128), f32),
@@ -268,6 +327,7 @@
             pltpu.VMEM((2, ROWS), f32),
             pltpu.VMEM((2, ROWS, F + R), bf16),
             pltpu.VMEM((2, 2, ROWS), f32),
+            pltpu.VMEM((PIECE, F + R), bf16),
             pltpu.VMEM((ROWS, F + R), bf16),
             pltpu.VMEM((2, ROWS), f32),
             pltpu.VMEM((CHUNKS, R, CHUNK), bf16),
@@ -275,12 +335,14 @@
             pltpu.VMEM((ROWS, R), f32),
             pltpu.VMEM((2 * sites, R), f32),
             pltpu.VMEM((ZS * CS, 4, R), f32),
-            pltpu.VMEM((YS * XS, 4, R), f32),
-            dma((3,)),
-            dma((2, CHUNKS)),
-            dma((2, CHUNKS)),
-            dma((2,)),
-            dma((2,)),
+            pltpu.VMEM((SPOTS, 4, R), f32),
+            dma((6,)),
+            dma((2,)),
+            dma((2,)),
+            dma((2,)),
+            dma((2,)),
+            dma,
+            dma,
             dma((CHUNKS,)),
             dma((CHUNKS,)),
             dma,
@@ -291,10 +353,10 @@
             dma((2,)),
         ],
         compiler_params=pltpu.CompilerParams(
-            collective_id=0, has_side_effects=True, vmem_limit_bytes=48 * 1024 * 1024
+            collective_id=0, has_side_effects=True, vmem_limit_bytes=56 * 1024 * 1024
         ),
         name="cg_products",
-    )(embeddings, direction, residual, site_ids.reshape(1, ROWS), inv_scale.reshape(1, F), noise.reshape(1, R))
+    )(embeddings, direction, residual, site_ids, inv_scale, noise)
     old_norms, curvature, mixed, applied_norms = sums
     step_size = old_norms / curvature
     new_norms = jnp.maximum(old_norms - 2.0 * step_size * mixed + step_size * step_size * applied_norms, 0.0)

time: 77.9 us -> 75.8 us (0.973)
  local copies, waits for them, and re-layouts: 4.54 us -> 0.68 us
  other arithmetic: 1.81 us -> 2.81 us
  Pallas kernels: 70.6 us -> 71.4 us
    unnamed x14 -> x8, local copies, waits for them, and re-layouts: 4.54 us -> 0.68 us
    add x1, other arithmetic: 1.27 us -> 2.27 us  [body(): new_direction = new_residual + new_norms / old_norms * direction]
    pallas_call x1, Pallas kernels: 70.6 us -> 71.4 us  [body(): pl.pallas_call(kernel, out_shape=(jax.ShapeDtypeStruct((ROWS, R), f32), j...]
where the time goes in v2:
time: 75.8 us; the launch traced here: 75.6 us
  Pallas kernels  71.4 us (94%)
  other arithmetic  2.81 us (4%)
    pallas_call x1, Pallas kernels, body(): pl.pallas_call(kernel, out_shape=(jax.ShapeDtypeStruct((ROWS, R), f32), j...  71.4 us
    add x1, other arithmetic, body(): new_direction = new_residual + new_norms / old_norms * direction  2.27 us

profile of v2, /device:TPU:1, one launch (start us, length us, event | category | flops | bytes accessed | tf_op | source)
XLA Modules:
  0.0 75.6 jit_solution(11613598482978814231)
XLA Ops:
  0.6 0.0 copy-start
  0.6 0.0 copy-start.1
  0.7 0.0 copy-start.2
  0.7 71.4 %cg_products.1 = (f32[1024,128]{1,0:T(8,128)}, f32[4,128]{1,0:T(4,128)}) custom-call(bf16[1024,384]{1,0:T(8,128)(2,1)} %emb_hbm.1, f32[1024,128]{1,0:T(8,128)} %dir_hbm.1, f32[1024,128]{1,0:T(8,128)} %res_hbm.1, s32[1024]{0:T(1024)} %ids_hbm.1, f32[384]{0:T(512)} %scale_hbm.1, f32[128]{0:T(128)} %noise_hbm.1), custom_call_target="tpu_custom_call" | custom-call | tf_op jit(solution)/shard_map/cg_products/pallas_call | solution.py:308
  72.1 0.0 copy-start.3
  72.1 0.7 copy-done.3
  72.8 0.5 fusion.1
  73.3 0.0 copy-done
  73.3 0.0 copy-done.1
  73.3 0.0 copy-done.2
  73.3 2.3 %multiply_add_fusion = (f32[1024,128]{1,0:T(8,128)}, f32[1024,128]{1,0:T(8,128)}, f32[1024,128]{1,0:T(8,128)}) fusion(f32[1024,128]{1,0:T(8,128)S(1)} %copy-done, f32[128]{0:T(128)S(1)} %get-tuple-element.10, f32[1024,128]{1,0:T(8,128)S(1)} %copy-done.1, f32[1024,128]{1,0:T(8,128)} %get-tuple-element.7, f32[128]{0:T(128)S(1)} %bitcast.24, ...), kind=kLoop, calls=%fused_computation | loop fusion | flops 786432 | bytes 3671040 | tf_op jit(solution)/shard_map/add | solution.py:365
  (1 shorter events, 0.0 us)
Async XLA Ops:
  0.6 72.7 %copy-start = (f32[1024,128]{1,0:T(8,128)S(1)}, f32[1024,128]{1,0:T(8,128)}, u32[]{:S(2)}) copy-start(f32[1024,128]{1,0:T(8,128)} %dir_hbm.1) | copy-start | bytes 1572868
  0.6 72.7 %copy-start.1 = (f32[1024,128]{1,0:T(8,128)S(1)}, f32[1024,128]{1,0:T(8,128)}, u32[]{:S(2)}) copy-start(f32[1024,128]{1,0:T(8,128)} %res_hbm.1) | copy-start | bytes 1572868
  0.7 72.7 %copy-start.2 = (f32[1024,128]{1,0:T(8,128)S(1)}, f32[1024,128]{1,0:T(8,128)}, u32[]{:S(2)}) copy-start(f32[1024,128]{1,0:T(8,128)} %param.11) | copy-start | bytes 1572868
  72.1 0.7 copy-start.3

commit v3 on v2

--- a/solution.py
+++ b/solution.py
@@ -21,8 +21,10 @@
 R = 128
 CHUNK = 256
 CHUNKS = ROWS // CHUNK
+LANES = 128
 SPOTS = YS * XS
 PIECE = ROWS // SPOTS
+PARTS = ((0, 256), (256, 256), (512, 256), (768, 128), (896, 128))
 f32 = jnp.float32
 bf16 = jnp.bfloat16
 
@@ -53,12 +55,12 @@
 
 def kernel(
     emb_hbm, dir_hbm, res_hbm, ids_hbm, scale_hbm, noise_hbm,
-    applied_ref, sums_ref,
+    applied_hbm, coef_hbm,
     emb, direction, residual, ids_ref, scale_ref, noise_ref, own, left, norm_col, dir_t, own_meta,
-    near, near_meta, relay, far, far_meta, ret_out, ret_in, acc, totals, first, second,
+    near, near_meta, relay, far, far_meta, ret_out, ret_in, acc, totals, sums_ref, coef_ref, first, second,
     load_sem, near_send, near_recv, near_meta_send, near_meta_recv,
     relay_send, relay_recv, far_send, far_recv, far_meta_send, far_meta_recv,
-    ret_send, ret_recv, sum_send, sum_recv,
+    ret_send, ret_recv, sum_send, sum_recv, out_sem, coef_sem,
 ):
     me = lax.axis_index("pts")
     core = me % CS
@@ -78,9 +80,9 @@
     def at_place(base, p, c):
         return base + (p + c * (SPOTS - 1 - 2 * p)) * CS + c
 
-    relays = [at_place(next_plane, p, 1 - core) for p in range(SPOTS)]
-    next_edge = relays[0]
-    own_edge = at_place(plane * PLANE, 0, core)
+    relays = [at_place(plane * PLANE, p, core) for p in range(SPOTS)]
+    next_relays = [at_place(next_plane, p, 1 - core) for p in range(SPOTS)]
+    own_edge, next_edge = relays[0], next_relays[0]
 
     column_place = plane * CS + core
     column = [
@@ -91,26 +93,34 @@
         plane * PLANE + ((spot + k) % SPOTS) * CS + core for k in range(1, SPOTS)
     ]
 
-    loads = [
-        pltpu.make_async_copy(src, dst, load_sem.at[k])
-        for k, (src, dst) in enumerate(
+    def load(k, src, dst):
+        copy = pltpu.make_async_copy(src, dst, load_sem.at[k])
+        copy.start()
+        return copy
+
+    scale_load = load(0, scale_hbm, scale_ref)
+    block_loads = []
+    for k in range(CHUNKS):
+        rows = pl.ds(k * CHUNK, CHUNK)
+        block_loads.append(
             (
-                (emb_hbm, emb), (dir_hbm, direction), (scale_hbm, scale_ref),
-                (ids_hbm, ids_ref), (noise_hbm, noise_ref), (res_hbm, residual),
+                load(4 + 2 * k, emb_hbm.at[rows], emb.at[rows]),
+                load(5 + 2 * k, dir_hbm.at[rows], direction.at[rows]),
             )
         )
-    ]
-    for load in loads:
-        load.start()
+    ids_load = load(1, ids_hbm, ids_ref)
+    noise_load = load(2, noise_hbm, noise_ref)
+    res_load = load(3, res_hbm, residual)
 
     barrier = pltpu.get_barrier_semaphore()
     partners = [beside] + column + layer
     for other in partners:
         pl.semaphore_signal(barrier, inc=1, device_id=(other,), device_id_type=MESH)
 
-    @pl.when(jnp.logical_not(at_edge))
-    def _():
-        pl.semaphore_signal(barrier, inc=1, device_id=(next_edge,), device_id_type=MESH)
+    @pl.when(at_edge)
+    def _():
+        for other in next_relays[1:]:
+            pl.semaphore_signal(barrier, inc=1, device_id=(other,), device_id_type=MESH)
 
     def send(src, dst, send_sem, recv_sem, other):
         return pltpu.make_async_remote_copy(
@@ -122,8 +132,11 @@
         return pl.ds(k * CHUNK, CHUNK)
 
     far_copies = [
-        send(own.at[rows_of(k)], far.at[rows_of(k)], far_send.at[k], far_recv.at[k], opposite)
-        for k in range(CHUNKS)
+        send(
+            own.at[pl.ds(first_row, size)], far.at[pl.ds(first_row, size)],
+            far_send.at[k], far_recv.at[k], opposite,
+        )
+        for k, (first_row, size) in enumerate(PARTS)
     ]
     twin_copies = [
         send(own.at[rows_of(k)], near.at[0, rows_of(k)], near_send.at[0], near_recv.at[0], twin)
@@ -147,36 +160,39 @@
         return send(own.at[piece_of(p)], relay, near_send.at[1], relay_recv, relays[p])
 
     held_rows = pl.ds(pl.multiple_of(place * PIECE, PIECE), PIECE)
-    relay_copy = send(relay, near.at[1, held_rows], relay_send, near_recv.at[1], own_edge)
+    relay_copy = send(relay, near.at[1, held_rows], relay_send, near_recv.at[1], next_edge)
     relay_in = send(relay, relay, relay_send, relay_recv, own_edge)
     far_meta_copy = send(own_meta, far_meta, far_meta_send, far_meta_recv, opposite)
     near_meta_copies = [
         send(own_meta, near_meta.at[n], near_meta_send.at[n], near_meta_recv.at[n], other)
         for n, other in enumerate((twin, beside))
     ]
+    def strips_of(first_row, size):
+        return pl.ds(first_row // LANES, size // LANES)
+
     ret_copies = [
-        send(ret_out.at[k], ret_in.at[k], ret_send.at[k], ret_recv.at[k], opposite)
-        for k in range(CHUNKS)
-    ]
-
-    for load in loads[:3]:
-        load.wait()
+        send(
+            ret_out.at[strips_of(*part)], ret_in.at[strips_of(*part)],
+            ret_send.at[k], ret_recv.at[k], opposite,
+        )
+        for k, part in enumerate(PARTS)
+    ]
+
+    scale_load.wait()
     for k in range(CHUNKS):
         rows = rows_of(k)
-        scaled = (emb[rows, :].astype(f32) * scale_ref[...].reshape(1, F)).astype(bf16)
-        own[rows, :F] = scaled
+        for copy in block_loads[k]:
+            copy.wait()
+        own[rows, :F] = (emb[rows, :].astype(f32) * scale_ref[...].reshape(1, F)).astype(bf16)
         own[rows, F:] = direction[rows, :].astype(bf16)
-        wide = scaled.astype(f32)
-        left[rows, :] = (-2.0 * wide).astype(bf16)
-        norm_col[rows, :] = jnp.broadcast_to(jnp.sum(wide * wide, axis=1, keepdims=True), (CHUNK, 128))
         if k == 0:
-            pl.semaphore_wait(barrier, len(partners) + jnp.where(at_edge, SPOTS - 1, 0))
+            pl.semaphore_wait(barrier, len(partners) + jnp.where(at_edge, 0, 1))
 
         @pl.when(sends)
         def _():
-            far_copies[k].start()
-
-        twin_copies[k].start()
+            for part, copy in zip(PARTS, far_copies):
+                if part[0] // CHUNK == k:
+                    copy.start()
 
         @pl.when(at_edge)
         def _():
@@ -187,7 +203,14 @@
         def _():
             beside_copies[k].start()
 
-    loads[3].wait()
+        twin_copies[k].start()
+
+    for k in range(CHUNKS):
+        rows = rows_of(k)
+        wide = own[rows, :F].astype(f32)
+        left[rows, :] = (-2.0 * wide).astype(bf16)
+        norm_col[rows, :] = jnp.broadcast_to(jnp.sum(wide * wide, axis=1, keepdims=True), (CHUNK, LANES))
+    ids_load.wait()
     own_meta[0:1, :] = norm_col[...].T[0:1, :]
     own_meta[1:2, :] = ids_ref[...].reshape(1, ROWS).astype(f32)
 
@@ -208,7 +231,7 @@
         lax.fori_loop(0, CHUNKS, some_rows, 0)
         return dot(one_hot(meta[1:2, :]), block[:, F:])
 
-    loads[4].wait()
+    noise_load.wait()
     acc[...] = noise_ref[...].reshape(1, R) * direction[...]
     dir_t[...] = direction[...].T.astype(bf16)
     own_totals = add_block(own, own_meta)
@@ -224,49 +247,55 @@
         relay_in.wait_recv()
         relay_copy.start()
 
-    def far_chunk(k):
+    def far_part(k):
         far_copies[k].wait_recv()
-        rows = rows_of(k)
+        first_row, size = PARTS[k]
+        rows = pl.ds(first_row, size)
         tile = matern(left[...], far[rows, :F], norm_col[:, 0:1], far_meta[0:1, rows])
         spots = one_hot(far_meta[1:2, rows])
         back = dot(dir_t[...], tile) + site_weight * dot(own_halves_t, spots)
-        ret_out[k] = back.astype(bf16)
+        for strip in range(size // LANES):
+            ret_out[first_row // LANES + strip] = back[:, strip * LANES:(strip + 1) * LANES].astype(bf16)
         ret_copies[k].start()
         acc[...] += dot(tile, far[rows, F:])
         totals[...] += dot(spots, far[rows, F:])
 
-    def take_back(k):
-        ret_copies[k].wait_recv()
-        acc[rows_of(k), :] += ret_in[k].astype(f32).T
+    def finish_rows(rows, size):
+        spread = one_hot(own_meta[1:2, rows]).astype(f32).T.astype(bf16)
+        applied = acc[rows, :] + site_weight * dot(spread, split_halves(totals[...]))
+        acc[rows, :] = applied
+        held, step_rows = residual[rows, :], direction[rows, :]
+        sums_ref[1:2, :] += jnp.sum(step_rows * applied, axis=0, keepdims=True)
+        sums_ref[2:3, :] += jnp.sum(held * applied, axis=0, keepdims=True)
+        sums_ref[3:4, :] += jnp.sum(applied * applied, axis=0, keepdims=True)
+        return pltpu.make_async_copy(acc.at[rows], applied_hbm.at[rows], out_sem)
 
     @pl.when(receives)
     def _():
         far_meta_copy.wait_recv()
-        far_chunk(0)
+        far_part(0)
 
     near_meta_copies[1].wait_recv()
     near_whole[1].wait_recv()
     totals[...] += add_block(near.at[1], near_meta.at[1])
 
-    loads[5].wait()
+    res_load.wait()
+    sums_ref[...] = jnp.zeros_like(sums_ref)
     sums_ref[0:1, :] = jnp.sum(residual[...] * residual[...], axis=0, keepdims=True)
 
     @pl.when(receives)
     def _():
-        for k in range(1, CHUNKS):
-            far_chunk(k)
+        for k in range(1, len(PARTS)):
+            far_part(k)
+        finish_rows(pl.ds(0, ROWS), ROWS).start()
 
     @pl.when(sends)
     def _():
-        for k in range(CHUNKS):
-            take_back(k)
-
-    spread = one_hot(own_meta[1:2, :]).astype(f32).T.astype(bf16)
-    applied = acc[...] + site_weight * dot(spread, split_halves(totals[...]))
-    applied_ref[...] = applied
-    sums_ref[1:2, :] = jnp.sum(direction[...] * applied, axis=0, keepdims=True)
-    sums_ref[2:3, :] = jnp.sum(residual[...] * applied, axis=0, keepdims=True)
-    sums_ref[3:4, :] = jnp.sum(applied * applied, axis=0, keepdims=True)
+        for k, (first_row, size) in enumerate(PARTS):
+            ret_copies[k].wait_recv()
+            for strip in range(first_row // LANES, (first_row + size) // LANES):
+                acc[pl.ds(strip * LANES, LANES), :] += ret_in[strip].astype(f32).T
+            finish_rows(pl.ds(first_row, size), size).start()
 
     def gather_sum(stage, slots, slot, others):
         slots[slot] = sums_ref[...]
@@ -279,6 +308,16 @@
         return every
 
     stages = [gather_sum(0, first, column_place, column), gather_sum(1, second, spot, layer)]
+    old_norms, curvature = sums_ref[0:1, :], sums_ref[1:2, :]
+    step_size = old_norms / curvature
+    new_norms = old_norms - 2.0 * step_size * sums_ref[2:3, :] + step_size * step_size * sums_ref[3:4, :]
+    new_norms = jnp.maximum(new_norms, 0.0)
+    coef_ref[0:1, :] = step_size
+    coef_ref[1:2, :] = new_norms / old_norms
+    coef_ref[2:3, :] = new_norms
+    coef_ref[3:4, :] = old_norms
+    coef_out = pltpu.make_async_copy(coef_ref, coef_hbm, coef_sem)
+    coef_out.start()
     for stage in stages:
         stage.wait_send()
 
@@ -299,20 +338,56 @@
 
     for copy in near_meta_copies + near_whole:
         copy.wait_send()
+    pltpu.make_async_copy(acc, applied_hbm, out_sem).wait()
+    coef_out.wait()
+
+
+def update(
+    sol_hbm, res_hbm, dir_hbm, applied_hbm, coef_hbm,
+    new_sol_hbm, new_res_hbm, new_dir_hbm, norms_hbm,
+    coef_ref, held, made, norms, in_sem, out_sem,
+):
+    def copy(src, dst, sem):
+        moving = pltpu.make_async_copy(src, dst, sem)
+        moving.start()
+        return moving
+
+    coef_in = copy(coef_hbm, coef_ref, in_sem.at[4 * CHUNKS])
+    loads, stores = [], []
+    for k in range(CHUNKS):
+        rows = pl.ds(k * CHUNK, CHUNK)
+        for n, src in enumerate((applied_hbm, res_hbm, dir_hbm, sol_hbm)):
+            loads.append(copy(src.at[rows], held.at[n, rows], in_sem.at[4 * k + n]))
+    coef_in.wait()
+    step_size, ratio = coef_ref[0:1, :], coef_ref[1:2, :]
+    norms[...] = coef_ref[2:3, :].reshape(R)
+    stores.append(copy(norms, norms_hbm, out_sem.at[3 * CHUNKS]))
+    for k in range(CHUNKS):
+        rows = pl.ds(k * CHUNK, CHUNK)
+        for n in range(4):
+            loads[4 * k + n].wait()
+        step_rows = held[2, rows, :]
+        moved = held[1, rows, :] - step_size * held[0, rows, :]
+        made[0, rows, :] = moved
+        made[1, rows, :] = held[3, rows, :] + step_size * step_rows
+        made[2, rows, :] = moved + ratio * step_rows
+        for n, out in enumerate((new_res_hbm, new_sol_hbm, new_dir_hbm)):
+            stores.append(copy(made.at[n, rows], out.at[rows], out_sem.at[3 * k + n]))
+    for store in stores:
+        store.wait()
 
 
 def body(embeddings, site_ids, inv_scale, noise, solution, residual, direction):
-    vmem = pl.BlockSpec(memory_space=pltpu.VMEM)
     hbm = pl.BlockSpec(memory_space=pltpu.HBM)
     dma = pltpu.SemaphoreType.DMA
-    applied, sums = pl.pallas_call(
+    applied, coefs = pl.pallas_call(
         kernel,
         out_shape=(
             jax.ShapeDtypeStruct((ROWS, R), f32),
             jax.ShapeDtypeStruct((4, R), f32),
         ),
         in_specs=[hbm] * 6,
-        out_specs=[vmem] * 2,
+        out_specs=[hbm] * 2,
         scratch_shapes=[
             pltpu.VMEM((ROWS, F), bf16),
             pltpu.VMEM((ROWS, R), f32),
@@ -330,39 +405,54 @@
             pltpu.VMEM((PIECE, F + R), bf16),
             pltpu.VMEM((ROWS, F + R), bf16),
             pltpu.VMEM((2, ROWS), f32),
-            pltpu.VMEM((CHUNKS, R, CHUNK), bf16),
-            pltpu.VMEM((CHUNKS, R, CHUNK), bf16),
+            pltpu.VMEM((ROWS // LANES, R, LANES), bf16),
+            pltpu.VMEM((ROWS // LANES, R, LANES), bf16),
             pltpu.VMEM((ROWS, R), f32),
             pltpu.VMEM((2 * sites, R), f32),
+            pltpu.VMEM((4, R), f32),
+            pltpu.VMEM((4, R), f32),
             pltpu.VMEM((ZS * CS, 4, R), f32),
             pltpu.VMEM((SPOTS, 4, R), f32),
-            dma((6,)),
-            dma((2,)),
-            dma((2,)),
-            dma((2,)),
-            dma((2,)),
-            dma,
-            dma,
-            dma((CHUNKS,)),
-            dma((CHUNKS,)),
-            dma,
-            dma,
-            dma((CHUNKS,)),
-            dma((CHUNKS,)),
-            dma((2,)),
-            dma((2,)),
+            dma((4 + 2 * CHUNKS,)),
+            dma((2,)),
+            dma((2,)),
+            dma((2,)),
+            dma((2,)),
+            dma,
+            dma,
+            dma((len(PARTS),)),
+            dma((len(PARTS),)),
+            dma,
+            dma,
+            dma((len(PARTS),)),
+            dma((len(PARTS),)),
+            dma((2,)),
+            dma((2,)),
+            dma,
+            dma,
         ],
         compiler_params=pltpu.CompilerParams(
             collective_id=0, has_side_effects=True, vmem_limit_bytes=56 * 1024 * 1024
         ),
         name="cg_products",
     )(embeddings, direction, residual, site_ids, inv_scale, noise)
-    old_norms, curvature, mixed, applied_norms = sums
-    step_size = old_norms / curvature
-    new_norms = jnp.maximum(old_norms - 2.0 * step_size * mixed + step_size * step_size * applied_norms, 0.0)
-    new_solution = solution + step_size * direction
-    new_residual = residual - step_size * applied
-    new_direction = new_residual + new_norms / old_norms * direction
+    block = jax.ShapeDtypeStruct((ROWS, R), f32)
+    new_solution, new_residual, new_direction, new_norms = pl.pallas_call(
+        update,
+        out_shape=(block, block, block, jax.ShapeDtypeStruct((R,), f32)),
+        in_specs=[hbm] * 5,
+        out_specs=[hbm] * 4,
+        scratch_shapes=[
+            pltpu.VMEM((4, R), f32),
+            pltpu.VMEM((4, ROWS, R), f32),
+            pltpu.VMEM((3, ROWS, R), f32),
+            pltpu.VMEM((R,), f32),
+            dma((4 * CHUNKS + 1,)),
+            dma((3 * CHUNKS + 1,)),
+        ],
+        compiler_params=pltpu.CompilerParams(vmem_limit_bytes=62 * 1024 * 1024),
+        name="cg_update",
+    )(solution, residual, direction, applied, coefs)
     return (new_solution, new_residual, new_direction, new_norms)
 
 

time: 75.8 us -> 65.7 us (0.87)
  Pallas kernels: 71.4 us -> 64.9 us
  other arithmetic: 2.81 us -> 0 us
    pallas_call x1, Pallas kernels: 71.4 us -> 62.3 us  [body(): pl.pallas_call(kernel, out_shape=(jax.ShapeDtypeStruct((ROWS, R), f32), j...]
    pallas_call x0 -> x1, Pallas kernels: none -> 2.64 us  [body(): pl.pallas_call(update, out_shape=(block, block, block, jax.ShapeDtypeStru...]
    add x1 -> x0, other arithmetic: 2.27 us -> none  [body(): new_direction = new_residual + new_norms / old_norms * direction]
where the time goes in v3:
time: 65.7 us; the launch traced here: 65.6 us
  Pallas kernels  64.9 us (99%)
    pallas_call x1, Pallas kernels, body(): pl.pallas_call(kernel, out_shape=(jax.ShapeDtypeStruct((ROWS, R), f32), j...  62.3 us
    pallas_call x1, Pallas kernels, body(): pl.pallas_call(update, out_shape=(block, block, block, jax.ShapeDtypeStru...  2.64 us

profile of v3, /device:TPU:1, one launch (start us, length us, event | category | flops | bytes accessed | tf_op | source)
XLA Modules:
  0.0 65.6 jit_solution(11931512994382399787)
XLA Ops:
  0.6 62.3 %cg_products.1 = (f32[1024,128]{1,0:T(8,128)}, f32[4,128]{1,0:T(4,128)}) custom-call(bf16[1024,384]{1,0:T(8,128)(2,1)} %emb_hbm.1, f32[1024,128]{1,0:T(8,128)} %dir_hbm.3, f32[1024,128]{1,0:T(8,128)} %res_hbm.3, s32[1024]{0:T(1024)} %ids_hbm.1, f32[384]{0:T(512)} %scale_hbm.1, f32[128]{0:T(128)} %noise_hbm.1), custom_call_target="tpu_custom_call" | custom-call | tf_op jit(solution)/shard_map/cg_products/pallas_call | solution.py:383
  62.9 2.6 %cg_update.1 = (f32[1024,128]{1,0:T(8,128)}, f32[1024,128]{1,0:T(8,128)}, f32[1024,128]{1,0:T(8,128)}, f32[128]{0:T(128)}) custom-call(f32[1024,128]{1,0:T(8,128)} %sol_hbm.1, f32[1024,128]{1,0:T(8,128)} %res_hbm.3, f32[1024,128]{1,0:T(8,128)} %dir_hbm.3, f32[1024,128]{1,0:T(8,128)} %get-tuple-element.6.applied_hbm, f32[4,128]{1,0:T(4,128)} %get-tuple-element.7.coef_hbm), custom_call_target="tpu_custom_call" | custom-call | tf_op jit(solution)/shard_map/cg_update/pallas_call | solution.py:440

commit v4 on v3

--- a/solution.py
+++ b/solution.py
@@ -55,12 +55,12 @@
 
 def kernel(
     emb_hbm, dir_hbm, res_hbm, ids_hbm, scale_hbm, noise_hbm,
-    applied_hbm, coef_hbm,
-    emb, direction, residual, ids_ref, scale_ref, noise_ref, own, left, norm_col, dir_t, own_meta,
-    near, near_meta, relay, far, far_meta, ret_out, ret_in, acc, totals, sums_ref, coef_ref, first, second,
+    acc, direction, residual, coef_ref,
+    emb, ids_ref, scale_ref, noise_ref, own, left, norm_col, dir_t, own_meta,
+    near, near_meta, relay, far, far_meta, ret_out, ret_in, totals, sums_ref, first, second,
     load_sem, near_send, near_recv, near_meta_send, near_meta_recv,
     relay_send, relay_recv, far_send, far_recv, far_meta_send, far_meta_recv,
-    ret_send, ret_recv, sum_send, sum_recv, out_sem, coef_sem,
+    ret_send, ret_recv, sum_send, sum_recv,
 ):
     me = lax.axis_index("pts")
     core = me % CS
@@ -85,12 +85,21 @@
     own_edge, next_edge = relays[0], next_relays[0]
 
     column_place = plane * CS + core
+    row, col = spot // XS, spot % XS
+
+    def turn(distance, size):
+        return min(distance, size - distance)
+
     column = [
         ((plane + dz) % ZS) * PLANE + spot * CS + (core + dc) % CS
-        for dz in range(ZS) for dc in range(CS) if dz or dc
+        for dz in sorted(range(ZS), key=lambda d: -turn(d, ZS)) for dc in range(CS) if dz or dc
     ]
     layer = [
-        plane * PLANE + ((spot + k) % SPOTS) * CS + core for k in range(1, SPOTS)
+        plane * PLANE + ((row + dy) % YS * XS + (col + dx) % XS) * CS + core
+        for dy, dx in sorted(
+            ((dy, dx) for dy in range(YS) for dx in range(XS) if dy or dx),
+            key=lambda d: -turn(d[0], YS) - turn(d[1], XS),
+        )
     ]
 
     def load(k, src, dst):
@@ -113,7 +122,7 @@
     res_load = load(3, res_hbm, residual)
 
     barrier = pltpu.get_barrier_semaphore()
-    partners = [beside] + column + layer
+    partners = [other for pair in zip(column, layer) for other in pair] + [beside]
     for other in partners:
         pl.semaphore_signal(barrier, inc=1, device_id=(other,), device_id_type=MESH)
 
@@ -238,14 +247,14 @@
     totals[...] = own_totals
     own_halves_t = split_halves(own_totals).astype(f32).T.astype(bf16)
 
+    @pl.when(jnp.logical_not(at_edge))
+    def _():
+        relay_in.wait_recv()
+        relay_copy.start()
+
     near_meta_copies[0].wait_recv()
     near_whole[0].wait_recv()
     totals[...] += add_block(near.at[0], near_meta.at[0])
-
-    @pl.when(jnp.logical_not(at_edge))
-    def _():
-        relay_in.wait_recv()
-        relay_copy.start()
 
     def far_part(k):
         far_copies[k].wait_recv()
@@ -260,7 +269,7 @@
         acc[...] += dot(tile, far[rows, F:])
         totals[...] += dot(spots, far[rows, F:])
 
-    def finish_rows(rows, size):
+    def finish_rows(rows):
         spread = one_hot(own_meta[1:2, rows]).astype(f32).T.astype(bf16)
         applied = acc[rows, :] + site_weight * dot(spread, split_halves(totals[...]))
         acc[rows, :] = applied
@@ -268,12 +277,13 @@
         sums_ref[1:2, :] += jnp.sum(step_rows * applied, axis=0, keepdims=True)
         sums_ref[2:3, :] += jnp.sum(held * applied, axis=0, keepdims=True)
         sums_ref[3:4, :] += jnp.sum(applied * applied, axis=0, keepdims=True)
-        return pltpu.make_async_copy(acc.at[rows], applied_hbm.at[rows], out_sem)
 
     @pl.when(receives)
     def _():
         far_meta_copy.wait_recv()
         far_part(0)
+        far_part(1)
+        far_part(2)
 
     near_meta_copies[1].wait_recv()
     near_whole[1].wait_recv()
@@ -285,9 +295,9 @@
 
     @pl.when(receives)
     def _():
-        for k in range(1, len(PARTS)):
+        for k in range(3, len(PARTS)):
             far_part(k)
-        finish_rows(pl.ds(0, ROWS), ROWS).start()
+        finish_rows(pl.ds(0, ROWS))
 
     @pl.when(sends)
     def _():
@@ -295,7 +305,7 @@
             ret_copies[k].wait_recv()
             for strip in range(first_row // LANES, (first_row + size) // LANES):
                 acc[pl.ds(strip * LANES, LANES), :] += ret_in[strip].astype(f32).T
-            finish_rows(pl.ds(first_row, size), size).start()
+            finish_rows(pl.ds(first_row, size))
 
     def gather_sum(stage, slots, slot, others):
         slots[slot] = sums_ref[...]
@@ -316,8 +326,6 @@
     coef_ref[1:2, :] = new_norms / old_norms
     coef_ref[2:3, :] = new_norms
     coef_ref[3:4, :] = old_norms
-    coef_out = pltpu.make_async_copy(coef_ref, coef_hbm, coef_sem)
-    coef_out.start()
     for stage in stages:
         stage.wait_send()
 
@@ -338,60 +346,51 @@
 
     for copy in near_meta_copies + near_whole:
         copy.wait_send()
-    pltpu.make_async_copy(acc, applied_hbm, out_sem).wait()
-    coef_out.wait()
 
 
 def update(
-    sol_hbm, res_hbm, dir_hbm, applied_hbm, coef_hbm,
+    sol_ref, res_ref, dir_ref, applied_ref, coef_ref,
     new_sol_hbm, new_res_hbm, new_dir_hbm, norms_hbm,
-    coef_ref, held, made, norms, in_sem, out_sem,
+    made, norms, out_sem,
 ):
-    def copy(src, dst, sem):
-        moving = pltpu.make_async_copy(src, dst, sem)
-        moving.start()
-        return moving
-
-    coef_in = copy(coef_hbm, coef_ref, in_sem.at[4 * CHUNKS])
-    loads, stores = [], []
+    stores = []
+
+    def store(src, dst, sem):
+        stores.append(pltpu.make_async_copy(src, dst, sem))
+        stores[-1].start()
+
+    step_size, ratio = coef_ref[0:1, :], coef_ref[1:2, :]
+    norms[...] = coef_ref[2:3, :].reshape(R)
+    store(norms, norms_hbm, out_sem.at[3 * CHUNKS])
     for k in range(CHUNKS):
         rows = pl.ds(k * CHUNK, CHUNK)
-        for n, src in enumerate((applied_hbm, res_hbm, dir_hbm, sol_hbm)):
-            loads.append(copy(src.at[rows], held.at[n, rows], in_sem.at[4 * k + n]))
-    coef_in.wait()
-    step_size, ratio = coef_ref[0:1, :], coef_ref[1:2, :]
-    norms[...] = coef_ref[2:3, :].reshape(R)
-    stores.append(copy(norms, norms_hbm, out_sem.at[3 * CHUNKS]))
-    for k in range(CHUNKS):
-        rows = pl.ds(k * CHUNK, CHUNK)
-        for n in range(4):
-            loads[4 * k + n].wait()
-        step_rows = held[2, rows, :]
-        moved = held[1, rows, :] - step_size * held[0, rows, :]
+        step_rows = dir_ref[rows, :]
+        moved = res_ref[rows, :] - step_size * applied_ref[rows, :]
         made[0, rows, :] = moved
-        made[1, rows, :] = held[3, rows, :] + step_size * step_rows
+        made[1, rows, :] = sol_ref[rows, :] + step_size * step_rows
         made[2, rows, :] = moved + ratio * step_rows
         for n, out in enumerate((new_res_hbm, new_sol_hbm, new_dir_hbm)):
-            stores.append(copy(made.at[n, rows], out.at[rows], out_sem.at[3 * k + n]))
-    for store in stores:
-        store.wait()
+            store(made.at[n, rows], out.at[rows], out_sem.at[3 * k + n])
+    for copy in stores:
+        copy.wait()
 
 
 def body(embeddings, site_ids, inv_scale, noise, solution, residual, direction):
     hbm = pl.BlockSpec(memory_space=pltpu.HBM)
+    vmem = pl.BlockSpec(memory_space=pltpu.VMEM)
     dma = pltpu.SemaphoreType.DMA
-    applied, coefs = pl.pallas_call(
+    applied, held_direction, held_residual, coefs = pl.pallas_call(
         kernel,
         out_shape=(
-            jax.ShapeDtypeStruct((ROWS, R), f32),
-            jax.ShapeDtypeStruct((4, R), f32),
+            pltpu.VMEM((ROWS, R), f32),
+            pltpu.VMEM((ROWS, R), f32),
+            pltpu.VMEM((ROWS, R), f32),
+            pltpu.VMEM((4, R), f32),
         ),
         in_specs=[hbm] * 6,
-        out_specs=[hbm] * 2,
+        out_specs=[vmem] * 4,
         scratch_shapes=[
             pltpu.VMEM((ROWS, F), bf16),
-            pltpu.VMEM((ROWS, R), f32),
-            pltpu.VMEM((ROWS, R), f32),
             pltpu.VMEM((ROWS,), jnp.int32),
             pltpu.VMEM((F,), f32),
             pltpu.VMEM((R,), f32),
@@ -407,9 +406,7 @@
             pltpu.VMEM((2, ROWS), f32),
             pltpu.VMEM((ROWS // LANES, R, LANES), bf16),
             pltpu.VMEM((ROWS // LANES, R, LANES), bf16),
-            pltpu.VMEM((ROWS, R), f32),
             pltpu.VMEM((2 * sites, R), f32),
-            pltpu.VMEM((4, R), f32),
             pltpu.VMEM((4, R), f32),
             pltpu.VMEM((ZS * CS, 4, R), f32),
             pltpu.VMEM((SPOTS, 4, R), f32),
@@ -428,8 +425,6 @@
             dma((len(PARTS),)),
             dma((2,)),
             dma((2,)),
-            dma,
-            dma,
         ],
         compiler_params=pltpu.CompilerParams(
             collective_id=0, has_side_effects=True, vmem_limit_bytes=56 * 1024 * 1024
@@ -440,19 +435,16 @@
     new_solution, new_residual, new_direction, new_norms = pl.pallas_call(
         update,
         out_shape=(block, block, block, jax.ShapeDtypeStruct((R,), f32)),
-        in_specs=[hbm] * 5,
+        in_specs=[vmem] * 5,
         out_specs=[hbm] * 4,
         scratch_shapes=[
-            pltpu.VMEM((4, R), f32),
-            pltpu.VMEM((4, ROWS, R), f32),
             pltpu.VMEM((3, ROWS, R), f32),
             pltpu.VMEM((R,), f32),
-            dma((4 * CHUNKS + 1,)),
             dma((3 * CHUNKS + 1,)),
         ],
-        compiler_params=pltpu.CompilerParams(vmem_limit_bytes=62 * 1024 * 1024),
+        compiler_params=pltpu.CompilerParams(vmem_limit_bytes=8 * 1024 * 1024),
         name="cg_update",
-    )(solution, residual, direction, applied, coefs)
+    )(solution, held_residual, held_direction, applied, coefs)
     return (new_solution, new_residual, new_direction, new_norms)
 
 

time: 65.7 us -> 62.6 us (0.953)
  Pallas kernels: 64.9 us -> 61.8 us
    pallas_call x1, Pallas kernels: 62.3 us -> 60.5 us  [body(): pl.pallas_call(kernel, out_shape=(pltpu.VMEM((ROWS, R), f32), pltpu.VMEM(...]
    pallas_call x1, Pallas kernels: 2.64 us -> 1.29 us  [body(): pl.pallas_call(update, out_shape=(block, block, block, jax.ShapeDtypeStru...]
where the time goes in v4:
time: 62.6 us; the launch traced here: 62.5 us
  Pallas kernels  61.8 us (99%)
  between operations  0.66 us (1%)
    pallas_call x1, Pallas kernels, body(): pl.pallas_call(kernel, out_shape=(pltpu.VMEM((ROWS, R), f32), pltpu.VMEM(...  60.5 us
    pallas_call x1, Pallas kernels, body(): pl.pallas_call(update, out_shape=(block, block, block, jax.ShapeDtypeStru...  1.29 us

profile of v4, /device:TPU:1, one launch (start us, length us, event | category | flops | bytes accessed | tf_op | source)
XLA Modules:
  0.0 62.5 jit_solution(15086547289005508820)
XLA Ops:
  0.6 0.0 copy-start
  0.6 60.5 %cg_products.1 = (f32[1024,128]{1,0:T(8,128)S(1)}, f32[1024,128]{1,0:T(8,128)S(1)}, f32[1024,128]{1,0:T(8,128)S(1)}, f32[4,128]{1,0:T(4,128)S(1)}) custom-call(bf16[1024,384]{1,0:T(8,128)(2,1)} %emb_hbm.1, f32[1024,128]{1,0:T(8,128)} %dir_hbm.1, f32[1024,128]{1,0:T(8,128)} %res_hbm.1, s32[1024]{0:T(1024)} %ids_hbm.1, f32[384]{0:T(512)} %scale_hbm.1, ...), custom_call_target="tpu_custom_call" | custom-call | tf_op jit(solution)/shard_map/cg_products/pallas_call | solution.py:382
  61.2 0.0 copy-done
  61.2 1.3 %cg_update.1 = (f32[1024,128]{1,0:T(8,128)}, f32[1024,128]{1,0:T(8,128)}, f32[1024,128]{1,0:T(8,128)}, f32[128]{0:T(128)}) custom-call(f32[1024,128]{1,0:T(8,128)S(1)} %copy-done, f32[1024,128]{1,0:T(8,128)S(1)} %get-tuple-element.8.res_ref, f32[1024,128]{1,0:T(8,128)S(1)} %get-tuple-element.9.dir_ref, f32[1024,128]{1,0:T(8,128)S(1)} %get-tuple-element.10.applied_ref, ...), custom_call_target="tpu_custom_call" | custom-call | tf_op jit(solution)/shard_map/cg_update/pallas_call | solution.py:435
Async XLA Ops:
  0.6 60.6 %copy-start = (f32[1024,128]{1,0:T(8,128)S(1)}, f32[1024,128]{1,0:T(8,128)}, u32[]{:S(2)}) copy-start(f32[1024,128]{1,0:T(8,128)} %sol_ref.1) | copy-start | bytes 1572868

commit v5 on v4

--- a/solution.py
+++ b/solution.py
@@ -57,7 +57,7 @@
     emb_hbm, dir_hbm, res_hbm, ids_hbm, scale_hbm, noise_hbm,
     acc, direction, residual, coef_ref,
     emb, ids_ref, scale_ref, noise_ref, own, left, norm_col, dir_t, own_meta,
-    near, near_meta, relay, far, far_meta, ret_out, ret_in, totals, sums_ref, first, second,
+    near, near_meta, relay, far, far_meta, ret_out, ret_in, totals, spread, sums_ref, first, second,
     load_sem, near_send, near_recv, near_meta_send, near_meta_recv,
     relay_send, relay_recv, far_send, far_recv, far_meta_send, far_meta_recv,
     ret_send, ret_recv, sum_send, sum_recv,
@@ -231,18 +231,14 @@
         copy.start()
 
     def add_block(block, meta):
-        def some_rows(t, carry):
-            rows = pl.ds(pl.multiple_of(t * CHUNK, CHUNK), CHUNK)
-            tile = matern(left[rows, :], block[:, :F], norm_col[rows, 0:1], meta[0:1, :])
-            acc[rows, :] += dot(tile, block[:, F:])
-            return carry
-
-        lax.fori_loop(0, CHUNKS, some_rows, 0)
+        tile = matern(left[...], block[:, :F], norm_col[:, 0:1], meta[0:1, :])
+        acc[...] += dot(tile, block[:, F:])
         return dot(one_hot(meta[1:2, :]), block[:, F:])
 
     noise_load.wait()
     acc[...] = noise_ref[...].reshape(1, R) * direction[...]
     dir_t[...] = direction[...].T.astype(bf16)
+    spread[...] = one_hot(own_meta[1:2, :]).astype(f32).T.astype(bf16)
     own_totals = add_block(own, own_meta)
     totals[...] = own_totals
     own_halves_t = split_halves(own_totals).astype(f32).T.astype(bf16)
@@ -256,7 +252,7 @@
     near_whole[0].wait_recv()
     totals[...] += add_block(near.at[0], near_meta.at[0])
 
-    def far_part(k):
+    def far_tile(k):
         far_copies[k].wait_recv()
         first_row, size = PARTS[k]
         rows = pl.ds(first_row, size)
@@ -266,12 +262,17 @@
         for strip in range(size // LANES):
             ret_out[first_row // LANES + strip] = back[:, strip * LANES:(strip + 1) * LANES].astype(bf16)
         ret_copies[k].start()
-        acc[...] += dot(tile, far[rows, F:])
-        totals[...] += dot(spots, far[rows, F:])
-
-    def finish_rows(rows):
-        spread = one_hot(own_meta[1:2, rows]).astype(f32).T.astype(bf16)
-        applied = acc[rows, :] + site_weight * dot(spread, split_halves(totals[...]))
+        return dot(tile, far[rows, F:]), dot(spots, far[rows, F:])
+
+    def far_part(k):
+        products, part_totals = far_tile(k)
+        acc[...] += products
+        totals[...] += part_totals
+
+    def add_sites():
+        acc[...] += site_weight * dot(spread[...], split_halves(totals[...]))
+
+    def add_sums(rows, applied):
         acc[rows, :] = applied
         held, step_rows = residual[rows, :], direction[rows, :]
         sums_ref[1:2, :] += jnp.sum(step_rows * applied, axis=0, keepdims=True)
@@ -295,17 +296,21 @@
 
     @pl.when(receives)
     def _():
-        for k in range(3, len(PARTS)):
+        for k in range(3, len(PARTS) - 1):
             far_part(k)
-        finish_rows(pl.ds(0, ROWS))
+        add_sites()
+        products, part_totals = far_tile(len(PARTS) - 1)
+        applied = acc[...] + products + site_weight * dot(spread[...], split_halves(part_totals))
+        add_sums(pl.ds(0, ROWS), applied)
 
     @pl.when(sends)
     def _():
+        add_sites()
         for k, (first_row, size) in enumerate(PARTS):
             ret_copies[k].wait_recv()
             for strip in range(first_row // LANES, (first_row + size) // LANES):
-                acc[pl.ds(strip * LANES, LANES), :] += ret_in[strip].astype(f32).T
-            finish_rows(pl.ds(first_row, size))
+                rows = pl.ds(strip * LANES, LANES)
+                add_sums(rows, acc[rows, :] + ret_in[strip].astype(f32).T)
 
     def gather_sum(stage, slots, slot, others):
         slots[slot] = sums_ref[...]
@@ -407,6 +412,7 @@
             pltpu.VMEM((ROWS // LANES, R, LANES), bf16),
             pltpu.VMEM((ROWS // LANES, R, LANES), bf16),
             pltpu.VMEM((2 * sites, R), f32),
+            pltpu.VMEM((ROWS, 2 * sites), bf16),
             pltpu.VMEM((4, R), f32),
             pltpu.VMEM((ZS * CS, 4, R), f32),
             pltpu.VMEM((SPOTS, 4, R), f32),

time: 62.6 us -> 61.5 us (0.982)
  Pallas kernels: 61.8 us -> 60.8 us
    pallas_call x1, Pallas kernels: 60.5 us -> 59.5 us  [body(): pl.pallas_call(kernel, out_shape=(pltpu.VMEM((ROWS, R), f32), pltpu.VMEM(...]
where the time goes in v5:
time: 61.5 us; the launch traced here: 61.4 us
  Pallas kernels  60.8 us (99%)
  between operations  0.66 us (1%)
    pallas_call x1, Pallas kernels, body(): pl.pallas_call(kernel, out_shape=(pltpu.VMEM((ROWS, R), f32), pltpu.VMEM(...  59.5 us
    pallas_call x1, Pallas kernels, body(): pl.pallas_call(update, out_shape=(block, block, block, jax.ShapeDtypeStru...  1.29 us

profile of v5, /device:TPU:1, one launch (start us, length us, event | category | flops | bytes accessed | tf_op | source)
XLA Modules:
  0.0 61.4 jit_solution(4838175158866356358)
XLA Ops:
  0.6 0.0 copy-start
  0.6 59.5 %cg_products.1 = (f32[1024,128]{1,0:T(8,128)S(1)}, f32[1024,128]{1,0:T(8,128)S(1)}, f32[1024,128]{1,0:T(8,128)S(1)}, f32[4,128]{1,0:T(4,128)S(1)}) custom-call(bf16[1024,384]{1,0:T(8,128)(2,1)} %emb_hbm.1, f32[1024,128]{1,0:T(8,128)} %dir_hbm.1, f32[1024,128]{1,0:T(8,128)} %res_hbm.1, s32[1024]{0:T(1024)} %ids_hbm.1, f32[384]{0:T(512)} %scale_hbm.1, ...), custom_call_target="tpu_custom_call" | custom-call | tf_op jit(solution)/shard_map/cg_products/pallas_call | solution.py:387
  60.1 0.0 copy-done
  60.1 1.3 %cg_update.1 = (f32[1024,128]{1,0:T(8,128)}, f32[1024,128]{1,0:T(8,128)}, f32[1024,128]{1,0:T(8,128)}, f32[128]{0:T(128)}) custom-call(f32[1024,128]{1,0:T(8,128)S(1)} %copy-done, f32[1024,128]{1,0:T(8,128)S(1)} %get-tuple-element.8.res_ref, f32[1024,128]{1,0:T(8,128)S(1)} %get-tuple-element.9.dir_ref, f32[1024,128]{1,0:T(8,128)S(1)} %get-tuple-element.10.applied_ref, ...), custom_call_target="tpu_custom_call" | custom-call | tf_op jit(solution)/shard_map/cg_update/pallas_call | solution.py:441
Async XLA Ops:
  0.6 59.5 %copy-start = (f32[1024,128]{1,0:T(8,128)S(1)}, f32[1024,128]{1,0:T(8,128)}, u32[]{:S(2)}) copy-start(f32[1024,128]{1,0:T(8,128)} %sol_ref.1) | copy-start | bytes 1572868

commit v6 on v5

--- a/solution.py
+++ b/solution.py
@@ -24,7 +24,7 @@
 LANES = 128
 SPOTS = YS * XS
 PIECE = ROWS // SPOTS
-PARTS = ((0, 256), (256, 256), (512, 256), (768, 128), (896, 128))
+PARTS = ((0, 384), (384, 384), (768, 256))
 f32 = jnp.float32
 bf16 = jnp.bfloat16
 
@@ -200,7 +200,7 @@
         @pl.when(sends)
         def _():
             for part, copy in zip(PARTS, far_copies):
-                if part[0] // CHUNK == k:
+                if (part[0] + part[1] - 1) // CHUNK == k:
                     copy.start()
 
         @pl.when(at_edge)
@@ -284,7 +284,6 @@
         far_meta_copy.wait_recv()
         far_part(0)
         far_part(1)
-        far_part(2)
 
     near_meta_copies[1].wait_recv()
     near_whole[1].wait_recv()
@@ -296,7 +295,7 @@
 
     @pl.when(receives)
     def _():
-        for k in range(3, len(PARTS) - 1):
+        for k in range(2, len(PARTS) - 1):
             far_part(k)
         add_sites()
         products, part_totals = far_tile(len(PARTS) - 1)

time: 61.5 us -> 60.6 us (0.985)
  Pallas kernels: 60.8 us -> 59.9 us
    pallas_call x1, Pallas kernels: 59.5 us -> 58.6 us  [body(): pl.pallas_call(kernel, out_shape=(pltpu.VMEM((ROWS, R), f32), pltpu.VMEM(...]
where the time goes in v6:
time: 60.6 us; the launch traced here: 60.5 us
  Pallas kernels  59.9 us (99%)
  between operations  0.66 us (1%)
    pallas_call x1, Pallas kernels, body(): pl.pallas_call(kernel, out_shape=(pltpu.VMEM((ROWS, R), f32), pltpu.VMEM(...  58.6 us
    pallas_call x1, Pallas kernels, body(): pl.pallas_call(update, out_shape=(block, block, block, jax.ShapeDtypeStru...  1.29 us

profile of v6, /device:TPU:1, one launch (start us, length us, event | category | flops | bytes accessed | tf_op | source)
XLA Modules:
  0.0 60.5 jit_solution(5212274781211605495)
XLA Ops:
  0.6 0.0 copy-start
  0.6 58.6 %cg_products.1 = (f32[1024,128]{1,0:T(8,128)S(1)}, f32[1024,128]{1,0:T(8,128)S(1)}, f32[1024,128]{1,0:T(8,128)S(1)}, f32[4,128]{1,0:T(4,128)S(1)}) custom-call(bf16[1024,384]{1,0:T(8,128)(2,1)} %emb_hbm.1, f32[1024,128]{1,0:T(8,128)} %dir_hbm.1, f32[1024,128]{1,0:T(8,128)} %res_hbm.1, s32[1024]{0:T(1024)} %ids_hbm.1, f32[384]{0:T(512)} %scale_hbm.1, ...), custom_call_target="tpu_custom_call" | custom-call | tf_op jit(solution)/shard_map/cg_products/pallas_call | solution.py:386
  59.2 0.0 copy-done
  59.3 1.3 %cg_update.1 = (f32[1024,128]{1,0:T(8,128)}, f32[1024,128]{1,0:T(8,128)}, f32[1024,128]{1,0:T(8,128)}, f32[128]{0:T(128)}) custom-call(f32[1024,128]{1,0:T(8,128)S(1)} %copy-done, f32[1024,128]{1,0:T(8,128)S(1)} %get-tuple-element.8.res_ref, f32[1024,128]{1,0:T(8,128)S(1)} %get-tuple-element.9.dir_ref, f32[1024,128]{1,0:T(8,128)S(1)} %get-tuple-element.10.applied_ref, ...), custom_call_target="tpu_custom_call" | custom-call | tf_op jit(solution)/shard_map/cg_update/pallas_call | solution.py:440
Async XLA Ops:
  0.6 58.6 %copy-start = (f32[1024,128]{1,0:T(8,128)S(1)}, f32[1024,128]{1,0:T(8,128)}, u32[]{:S(2)}) copy-start(f32[1024,128]{1,0:T(8,128)} %sol_ref.1) | copy-start | bytes 1572868

commit v7 on v4

--- a/solution.py
+++ b/solution.py
@@ -57,7 +57,7 @@
     emb_hbm, dir_hbm, res_hbm, ids_hbm, scale_hbm, noise_hbm,
     acc, direction, residual, coef_ref,
     emb, ids_ref, scale_ref, noise_ref, own, left, norm_col, dir_t, own_meta,
-    near, near_meta, relay, far, far_meta, ret_out, ret_in, totals, sums_ref, first, second,
+    near, near_meta, relay, far, far_meta, ret_out, ret_in, totals, spread, sums_ref, first, second,
     load_sem, near_send, near_recv, near_meta_send, near_meta_recv,
     relay_send, relay_recv, far_send, far_recv, far_meta_send, far_meta_recv,
     ret_send, ret_recv, sum_send, sum_recv,
@@ -200,7 +200,7 @@
         @pl.when(sends)
         def _():
             for part, copy in zip(PARTS, far_copies):
-                if part[0] // CHUNK == k:
+                if (part[0] + part[1] - 1) // CHUNK == k:
                     copy.start()
 
         @pl.when(at_edge)
@@ -232,17 +232,18 @@
 
     def add_block(block, meta):
         def some_rows(t, carry):
-            rows = pl.ds(pl.multiple_of(t * CHUNK, CHUNK), CHUNK)
+            rows = pl.ds(pl.multiple_of(t * 256, 256), 256)
             tile = matern(left[rows, :], block[:, :F], norm_col[rows, 0:1], meta[0:1, :])
             acc[rows, :] += dot(tile, block[:, F:])
             return carry
 
-        lax.fori_loop(0, CHUNKS, some_rows, 0)
+        lax.fori_loop(0, ROWS // 256, some_rows, 0)
         return dot(one_hot(meta[1:2, :]), block[:, F:])
 
     noise_load.wait()
     acc[...] = noise_ref[...].reshape(1, R) * direction[...]
     dir_t[...] = direction[...].T.astype(bf16)
+    spread[...] = one_hot(own_meta[1:2, :]).astype(f32).T.astype(bf16)
     own_totals = add_block(own, own_meta)
     totals[...] = own_totals
     own_halves_t = split_halves(own_totals).astype(f32).T.astype(bf16)
@@ -257,21 +258,23 @@
     totals[...] += add_block(near.at[0], near_meta.at[0])
 
     def far_part(k):
-        far_copies[k].wait_recv()
         first_row, size = PARTS[k]
         rows = pl.ds(first_row, size)
+        spots = one_hot(far_meta[1:2, rows])
+        back_sites = site_weight * dot(own_halves_t, spots)
+        far_copies[k].wait_recv()
         tile = matern(left[...], far[rows, :F], norm_col[:, 0:1], far_meta[0:1, rows])
-        spots = one_hot(far_meta[1:2, rows])
-        back = dot(dir_t[...], tile) + site_weight * dot(own_halves_t, spots)
+        back = dot(dir_t[...], tile) + back_sites
         for strip in range(size // LANES):
             ret_out[first_row // LANES + strip] = back[:, strip * LANES:(strip + 1) * LANES].astype(bf16)
         ret_copies[k].start()
         acc[...] += dot(tile, far[rows, F:])
         totals[...] += dot(spots, far[rows, F:])
 
-    def finish_rows(rows):
-        spread = one_hot(own_meta[1:2, rows]).astype(f32).T.astype(bf16)
-        applied = acc[rows, :] + site_weight * dot(spread, split_halves(totals[...]))
+    def add_sites():
+        acc[...] += site_weight * dot(spread[...], split_halves(totals[...]))
+
+    def add_sums(rows, applied):
         acc[rows, :] = applied
         held, step_rows = residual[rows, :], direction[rows, :]
         sums_ref[1:2, :] += jnp.sum(step_rows * applied, axis=0, keepdims=True)
@@ -281,9 +284,8 @@
     @pl.when(receives)
     def _():
         far_meta_copy.wait_recv()
-        far_part(0)
-        far_part(1)
-        far_part(2)
+        for k in range(len(PARTS)):
+            far_part(k)
 
     near_meta_copies[1].wait_recv()
     near_whole[1].wait_recv()
@@ -292,20 +294,19 @@
     res_load.wait()
     sums_ref[...] = jnp.zeros_like(sums_ref)
     sums_ref[0:1, :] = jnp.sum(residual[...] * residual[...], axis=0, keepdims=True)
+    add_sites()
 
     @pl.when(receives)
     def _():
-        for k in range(3, len(PARTS)):
-            far_part(k)
-        finish_rows(pl.ds(0, ROWS))
+        add_sums(pl.ds(0, ROWS), acc[...])
 
     @pl.when(sends)
     def _():
         for k, (first_row, size) in enumerate(PARTS):
             ret_copies[k].wait_recv()
             for strip in range(first_row // LANES, (first_row + size) // LANES):
-                acc[pl.ds(strip * LANES, LANES), :] += ret_in[strip].astype(f32).T
-            finish_rows(pl.ds(first_row, size))
+                rows = pl.ds(strip * LANES, LANES)
+                add_sums(rows, acc[rows, :] + ret_in[strip].astype(f32).T)
 
     def gather_sum(stage, slots, slot, others):
         slots[slot] = sums_ref[...]
@@ -407,6 +408,7 @@
             pltpu.VMEM((ROWS // LANES, R, LANES), bf16),
             pltpu.VMEM((ROWS // LANES, R, LANES), bf16),
             pltpu.VMEM((2 * sites, R), f32),
+            pltpu.VMEM((ROWS, 2 * sites), bf16),
             pltpu.VMEM((4, R), f32),
             pltpu.VMEM((ZS * CS, 4, R), f32),
             pltpu.VMEM((SPOTS, 4, R), f32),

time: 62.6 us -> 60.4 us (0.965)
  Pallas kernels: 61.8 us -> 59.7 us
    pallas_call x1, Pallas kernels: 60.5 us -> 58.4 us  [body(): pl.pallas_call(kernel, out_shape=(pltpu.VMEM((ROWS, R), f32), pltpu.VMEM(...]
where the time goes in v7:
time: 60.4 us; the launch traced here: 60.3 us
  Pallas kernels  59.7 us (99%)
  between operations  0.66 us (1%)
    pallas_call x1, Pallas kernels, body(): pl.pallas_call(kernel, out_shape=(pltpu.VMEM((ROWS, R), f32), pltpu.VMEM(...  58.4 us
    pallas_call x1, Pallas kernels, body(): pl.pallas_call(update, out_shape=(block, block, block, jax.ShapeDtypeStru...  1.29 us

profile of v7, /device:TPU:1, one launch (start us, length us, event | category | flops | bytes accessed | tf_op | source)
XLA Modules:
  0.0 60.3 jit_solution(6166934737470435274)
XLA Ops:
  0.6 0.0 copy-start
  0.6 58.4 %cg_products.1 = (f32[1024,128]{1,0:T(8,128)S(1)}, f32[1024,128]{1,0:T(8,128)S(1)}, f32[1024,128]{1,0:T(8,128)S(1)}, f32[4,128]{1,0:T(4,128)S(1)}) custom-call(bf16[1024,384]{1,0:T(8,128)(2,1)} %emb_hbm.1, f32[1024,128]{1,0:T(8,128)} %dir_hbm.1, f32[1024,128]{1,0:T(8,128)} %res_hbm.1, s32[1024]{0:T(1024)} %ids_hbm.1, f32[384]{0:T(512)} %scale_hbm.1, ...), custom_call_target="tpu_custom_call" | custom-call | tf_op jit(solution)/shard_map/cg_products/pallas_call | solution.py:383
  59.0 0.0 copy-done
  59.1 1.3 %cg_update.1 = (f32[1024,128]{1,0:T(8,128)}, f32[1024,128]{1,0:T(8,128)}, f32[1024,128]{1,0:T(8,128)}, f32[128]{0:T(128)}) custom-call(f32[1024,128]{1,0:T(8,128)S(1)} %copy-done, f32[1024,128]{1,0:T(8,128)S(1)} %get-tuple-element.8.res_ref, f32[1024,128]{1,0:T(8,128)S(1)} %get-tuple-element.9.dir_ref, f32[1024,128]{1,0:T(8,128)S(1)} %get-tuple-element.10.applied_ref, ...), custom_call_target="tpu_custom_call" | custom-call | tf_op jit(solution)/shard_map/cg_update/pallas_call | solution.py:437
Async XLA Ops:
  0.6 58.4 %copy-start = (f32[1024,128]{1,0:T(8,128)S(1)}, f32[1024,128]{1,0:T(8,128)}, u32[]{:S(2)}) copy-start(f32[1024,128]{1,0:T(8,128)} %sol_ref.1) | copy-start | bytes 1572868
